TPU v7x, 32 devices: a whole 2x2x4 slice. The times are simulated.
32 devices in a mesh: seq: 8 (over y, x, core), img: 4 (over z).
Axes of the slice: x: 2, y: 2, z: 4, core: 2. Of those that a mesh axis runs over, the one named last changes fastest.
Arguments:
- images: bfloat16 [8, 3072, 1024], P('img', 'seq'), may hold values from -6 to 6
- cotangent: bfloat16 [8, 3072, 1024], P('img', 'seq'), may hold values from -6 to 6
- attention_weight: float32 [4, 1024, 1024], P(None, ('seq', 'img')), as said below
- feedforward_weight: float32 [2, 1024, 4096], P(None, ('seq', 'img')), as said below
- norm_vectors: float32 [4, 1024], P(None, ('seq', 'img')), as said below
- attention_moment: float32 [4, 1024, 1024], P(None, ('seq', 'img')), may hold values from -0.00018310547 to 0.00018310547
- feedforward_moment: float32 [2, 1024, 4096], P(None, ('seq', 'img')), may hold values from -0.00018310547 to 0.00018310547
- norm_moment: float32 [4, 1024], P(None, ('seq', 'img')), may hold values from -0.00048828125 to 0.00048828125
- attention_second: float32 [4, 1024, 1024], P(None, ('seq', 'img')), may hold values from 2.38341e-09 to 3.17788e-08
- feedforward_second: float32 [2, 1024, 4096], P(None, ('seq', 'img')), may hold values from 2.38341e-09 to 3.17788e-08
- norm_second: float32 [4, 1024], P(None, ('seq', 'img')), may hold values from 2.145069e-08 to 2.860092e-07
- attention_average: float32 [4, 1024, 1024], P(None, ('seq', 'img')), may hold values from -0.1875 to 0.1875
- feedforward_average: float32 [2, 1024, 4096], P(None, ('seq', 'img')), may hold values from -0.1875 to 0.1875
- norm_average: float32 [4, 1024], P(None, ('seq', 'img')), may hold values from 0.5 to 1.5
Outputs:
- output: bfloat16 [8, 3072, 1024], P('img', 'seq')
- input_grad: bfloat16 [8, 3072, 1024], P('img', 'seq')
- grad_norm: float32 [], replicated
- new_attention: float32 [4, 1024, 1024], P(None, ('seq', 'img'))
- new_attention_moment: float32 [4, 1024, 1024], P(None, ('seq', 'img'))
- new_attention_second: float32 [4, 1024, 1024], P(None, ('seq', 'img'))
- new_attention_average: float32 [4, 1024, 1024], P(None, ('seq', 'img'))
- new_feedforward: float32 [2, 1024, 4096], P(None, ('seq', 'img'))
- new_feedforward_moment: float32 [2, 1024, 4096], P(None, ('seq', 'img'))
- new_feedforward_second: float32 [2, 1024, 4096], P(None, ('seq', 'img'))
- new_feedforward_average: float32 [2, 1024, 4096], P(None, ('seq', 'img'))
- new_norm: float32 [4, 1024], P(None, ('seq', 'img'))
- new_norm_moment: float32 [4, 1024], P(None, ('seq', 'img'))
- new_norm_second: float32 [4, 1024], P(None, ('seq', 'img'))
- new_norm_average: float32 [4, 1024], P(None, ('seq', 'img'))
Inputs may be any that keep to these rules, and one draw needn't show every extreme that they name: `attention_weight`: float32 master weights. `feedforward_weight`: float32 master weights. `norm_vectors`: gains are positive.
All inputs are finite; a program needn't handle non-finite values.
Results may differ from a plain program's by a relative error of at most 0.009.
Values may be sent and summed in bfloat16 or wider, within the bound.
No kernel may reach another device: no remote copies, remote signals or barrier semaphores. Data moves between devices by JAX's collectives and lax.ppermute only.
A program may use at most 256 MiB of HBM per device.

v0:
```python
import functools

import jax
import jax.numpy as jnp
import numpy as np
from jax import lax
from jax.experimental import pallas as pl
from jax.experimental.pallas import tpu as pltpu
from jax.sharding import PartitionSpec as P

HEADS = 16
HEAD_DIM = 64
STEP = 10

beta_first = 0.9
beta_second = 0.95
learn_rate = 0.02
norm_rate = 0.2
weight_decay = 0.1
average_decay = 0.75
clip_bound = 1.0
eps_norm = 1e-05
eps_adam = 1e-08

PAIR = 2 * HEAD_DIM
STATE_ROWS = HEAD_DIM + 16
SLAB = 1024
FEED_TILE = 1024
GROUP = 256

low = jnp.bfloat16
wide = jnp.float32


def params(megabytes=56):
    return pltpu.CompilerParams(vmem_limit_bytes=megabytes * 1024 * 1024)


def cost(products, elements):
    return pl.CostEstimate(flops=2 * products, bytes_accessed=elements, transcendentals=0)


def launch(kernel, tokens, in_specs, megabytes=56, **keys):
    known, extra = len(in_specs), len(tokens)

    def run(*refs):
        kernel(*refs[:known], *refs[known + extra :])

    call = pl.pallas_call(
        run, in_specs=list(in_specs) + [pl.BlockSpec(memory_space=pl.ANY)] * extra, compiler_params=params(megabytes), **keys
    )
    return lambda *args: call(*args, *tokens)


def launch_at(kernel, spot, tokens, grid, in_specs, out_specs, megabytes=56, scratch_shapes=(), **keys):
    known, extra = len(in_specs), len(tokens)

    def run(spot_ref, *refs):
        kernel(spot_ref, *refs[:known], *refs[known + extra :])

    call = pl.pallas_call(
        run,
        grid_spec=pltpu.PrefetchScalarGridSpec(
            num_scalar_prefetch=1,
            grid=grid,
            in_specs=list(in_specs) + [pl.BlockSpec(memory_space=pl.ANY)] * extra,
            out_specs=out_specs,
            scratch_shapes=scratch_shapes,
        ),
        compiler_params=params(megabytes),
        **keys,
    )
    return lambda *args: call(spot.reshape(-1).astype(jnp.int32), *args, *tokens)


def reversed_bits(value, count):
    return sum(((value >> k) & 1) << (count - 1 - k) for k in range(count))


def join(target_ref, bits, spot_ref, own_ref, came_ref, own_other_ref, came_other_ref):
    core, high, lowest = spot_ref[0], spot_ref[1], spot_ref[2]
    runs = 1 << (bits - 1)
    rows = target_ref.shape[1] // (2 * runs)
    for run in range(runs):
        source = slice(run * rows, (run + 1) * rows)
        turned = reversed_bits(run, bits)
        for place in range(2):
            first = (high ^ place) * runs + run
            second = turned + (lowest ^ place)
            for ref, slot in (((own_ref, came_ref)[place], core), ((own_other_ref, came_other_ref)[place], 1 - core)):
                at = jnp.where(slot == 0, first, second)
                target_ref[slot, pl.ds(pl.multiple_of(at * rows, rows), rows), :] = ref[source, :]


class Pieces:
    def __init__(self, arrays):
        self.arrays = [array.reshape(array.shape[0], -1, array.shape[-1]) for array in arrays]
        place = pos_index()
        self.bits = pos_bits()
        self.spot = jnp.stack([core_index(), place >> (self.bits - 1), place & 1])

    def blocks(self, columns, place):
        rows = self.arrays[0].shape[1]
        return [pl.BlockSpec((None, rows, columns), place)] * 4

    def second(self, columns):
        mine, others = (
            [part[0, :, columns].reshape(1 << (self.bits - 1), 1, -1, columns.stop - columns.start) for part in pair]
            for pair in (self.arrays[:2], self.arrays[2:])
        )
        own, came = (jnp.where(core_index() == 1, left, right) for left, right in zip(mine, others))
        straight, turned = jnp.concatenate([own, came], axis=1), jnp.concatenate([came, own], axis=1)
        runs = jnp.where(self.spot[2] == 0, straight, turned)
        order = [reversed_bits(run, self.bits - 1) for run in range(1 << (self.bits - 1))]
        return jnp.stack([runs[run] for run in order]).reshape(-1, columns.stop - columns.start)


def shaped(shape, kind):
    return jax.ShapeDtypeStruct(shape, kind)


def whole(shape):
    return pl.BlockSpec(shape, lambda *_: (0,) * len(shape))


def mm(left, right):
    return lax.dot_general(left, right, (((1,), (0,)), ((), ())), preferred_element_type=wide)


def mt(left, right):
    return lax.dot_general(left, right, (((1,), (1,)), ((), ())), preferred_element_type=wide)


def tm(left, right):
    return lax.dot_general(left, right, (((0,), (0,)), ((), ())), preferred_element_type=wide)


def pair_mm(first, second):
    if first[0].shape[1] % 128:
        return mm(*first) + mm(*second)
    return mm(jnp.concatenate([first[0], second[0]], axis=1), jnp.concatenate([first[1], second[1]], axis=0))


def causal_mask(span, below):
    rows = lax.broadcasted_iota(jnp.int32, (span, span), 0)
    columns = lax.broadcasted_iota(jnp.int32, (span, span), 1)
    return (rows >= columns if below else rows <= columns).astype(wide).astype(low)


def first_head(rows):
    return lax.broadcasted_iota(jnp.int32, (rows, PAIR), 1) < HEAD_DIM


def fold_state(product):
    return jnp.where(first_head(HEAD_DIM), product[:HEAD_DIM], product[HEAD_DIM:])


def unfold_state(folded):
    own = first_head(HEAD_DIM)
    zero = jnp.zeros_like(folded)
    return jnp.concatenate([jnp.where(own, folded, zero), jnp.where(own, zero, folded)], axis=0)


def unfold_total(row):
    tall = jnp.broadcast_to(row, (PAIR, PAIR))
    lanes = lax.broadcasted_iota(jnp.int32, (PAIR, PAIR), 1) < HEAD_DIM
    rows = lax.broadcasted_iota(jnp.int32, (PAIR, PAIR), 0) < HEAD_DIM
    return jnp.where(lanes == rows, tall, jnp.zeros_like(tall))


def split_low(values):
    high = values.astype(low)
    return high, (values - high.astype(wide)).astype(low)


def normalised(values):
    centre = jnp.mean(values, axis=-1, keepdims=True)
    centred = values - centre
    spread = jnp.mean(centred * centred, axis=-1, keepdims=True)
    scale = lax.rsqrt(spread + eps_norm)
    return centred * scale, scale


def feature(raw):
    return jnp.where(raw > 0, raw + 1.0, jnp.exp(jnp.minimum(raw, 0.0))).astype(low)


def project_kernel(images, span, bits, spot_ref, x_ref, vec_ref, *refs):
    fk_ref, v_ref, a_ref, at_ref, state_ref, wk_ref, wv_ref, joined_ref = refs[4:]

    @pl.when(pl.program_id(0) == 0)
    def _():
        gain, shift = vec_ref[0:1, :], vec_ref[1:2, :]
        step = span // 3
        for start in range(0, images * span, step):
            rows = slice(start, start + step)
            unit, _ = normalised(x_ref[rows, :].astype(wide))
            a_ref[rows, :] = (unit * gain + shift).astype(low)
        at_ref[...] = a_ref[...].T

    join(joined_ref, bits, spot_ref, *refs[:4])
    keys, values = joined_ref[0], joined_ref[1]
    wk_ref[...] = keys
    wv_ref[...] = values
    fk_ref[...] = feature(mm(a_ref[...], keys))
    v_ref[...] = mm(a_ref[...], values).astype(low)
    ones = jnp.ones((16, span), low)
    for image in range(images):
        rows = slice(image * span, (image + 1) * span)
        for pair in range(GROUP // PAIR):
            lanes = slice(pair * PAIR, (pair + 1) * PAIR)
            key, value = fk_ref[rows, lanes], v_ref[rows, lanes]
            state_ref[image, pair, :HEAD_DIM, :] = fold_state(tm(value, key))
            state_ref[image, pair, HEAD_DIM:, :] = mm(ones, key)


def project(x, vec, pieces, images, span, tokens=()):
    count, width = x.shape
    pairs = GROUP // PAIR
    column = pl.BlockSpec((count, GROUP), lambda g, spot: (0, g))
    weight = pl.BlockSpec((width, GROUP), lambda g, spot: (0, g))
    return launch_at(
        functools.partial(project_kernel, images, span, pieces.bits),
        pieces.spot,
        tokens,
        grid=(width // GROUP,),
        in_specs=[whole((count, width)), whole(vec.shape)] + pieces.blocks(GROUP, lambda g, spot: (0, 0, g)),
        out_specs=[
            column,
            column,
            whole((count, width)),
            whole((width, count)),
            pl.BlockSpec((images, pairs, STATE_ROWS, PAIR), lambda g, spot: (0, g, 0, 0)),
            weight,
            weight,
        ],
        out_shape=[
            shaped((count, width), low),
            shaped((count, width), low),
            shaped((count, width), low),
            shaped((width, count), low),
            shaped((images, width // PAIR, STATE_ROWS, PAIR), wide),
            shaped((width, width), low),
            shaped((width, width), low),
        ],
        scratch_shapes=[pltpu.VMEM((2, width, GROUP), low)],
        cost_estimate=cost(2 * count * width * width, 8 * width * width + 12 * count * width),
        name="project",
    )(x, vec, *pieces.arrays)


def query_kernel(bits, spot_ref, a_ref, *refs):
    fq_ref, wq_ref, wo_ref, joined_ref = refs[4:]
    join(joined_ref, bits, spot_ref, *refs[:4])
    wq_ref[...] = joined_ref[0]
    wo_ref[...] = joined_ref[1]
    fq_ref[...] = feature(mm(a_ref[...], joined_ref[0]))


def query(a, pieces, tokens=()):
    count, width = a.shape
    weight = pl.BlockSpec((width, GROUP), lambda g, spot: (0, g))
    return launch_at(
        functools.partial(query_kernel, pieces.bits),
        pieces.spot,
        tokens,
        grid=(width // GROUP,),
        in_specs=[whole((count, width))] + pieces.blocks(GROUP, lambda g, spot: (1, 0, g)),
        out_specs=[pl.BlockSpec((count, GROUP), lambda g, spot: (0, g)), weight, weight],
        out_shape=[shaped((count, width), low)] + [shaped((width, width), low)] * 2,
        scratch_shapes=[pltpu.VMEM((2, width, GROUP), low)],
        cost_estimate=cost(count * width * width, 6 * width * width + 4 * count * width),
        name="query",
    )(a, *pieces.arrays)


def turn_kernel(x_ref, out_ref):
    out_ref[...] = x_ref[...].T


def turn(x, images, span, tokens=()):
    count, width = x.shape
    return turned_whole(
        launch(
            turn_kernel,
            tokens,
            grid=(images,),
            in_specs=[pl.BlockSpec((span, width), lambda b: (b, 0))],
            out_specs=turned_block(width, span),
            out_shape=turned_shape(images, width, span),
            cost_estimate=cost(1, 4 * count * width),
                name="turn",
        )(x)
    )


def attend_kernel(span, fq_ref, fk_ref, v_ref, num_ref, den_ref):
    own = first_head(span)
    causal = causal_mask(span, True)
    one = jnp.ones((span, PAIR), low)
    zero = jnp.zeros((span, PAIR), low)
    for pair in range(GROUP // PAIR):
        lanes = slice(pair * PAIR, (pair + 1) * PAIR)
        query, key, value = fq_ref[:, lanes], fk_ref[:, lanes], v_ref[:, lanes]
        products = []
        for mask in (own, jnp.logical_not(own)):
            scores = mt(jnp.where(mask, query, zero), key).astype(low) * causal
            right = jnp.concatenate([jnp.where(mask, value, zero), jnp.where(mask, one, zero)], axis=1)
            products.append((scores, right))
        total = pair_mm(*products)
        num_ref[:, lanes] = total[:, :PAIR]
        den_ref[:, lanes] = total[:, PAIR:]


def attend(fq, fk, v, images, span, tokens=()):
    rows, width = fq.shape
    block = pl.BlockSpec((span, GROUP), lambda b, p: (b, p))
    return launch(
        functools.partial(attend_kernel, span),
        tokens,
        grid=(images, width // GROUP),
        in_specs=[block] * 3,
        out_specs=[block] * 2,
        out_shape=[shaped((rows, width), wide)] * 2,
        cost_estimate=cost(16 * rows * span * width, 14 * rows * width),
        name="attend",
    )(fq, fk, v)


def turned_block(width, span):
    if span % 128:
        return pl.BlockSpec((None, width, span), lambda b: (b, 0, 0))
    return pl.BlockSpec((width, span), lambda b: (0, b))


def turned_shape(images, width, span):
    return shaped((images, width, span) if span % 128 else (width, images * span), low)


def turned_whole(array):
    if array.ndim == 2:
        return array
    return jnp.swapaxes(array, 0, 1).reshape(array.shape[1], -1)


def mix_kernel(x_ref, vec_ref, wo_ref, fq_ref, num_ref, den_ref, prior_ref, mixed_ref, rden_ref, resid_ref, a_ref, at_ref, mt_ref):
    width = x_ref.shape[1]
    for pair in range(width // PAIR):
        lanes = slice(pair * PAIR, (pair + 1) * PAIR)
        folded = prior_ref[0, pair]
        matrix = jnp.concatenate(
            [unfold_state(folded[:HEAD_DIM]), unfold_total(folded[HEAD_DIM : HEAD_DIM + 1])], axis=0
        )
        high, rest = split_low(matrix)
        query = fq_ref[:, lanes]
        both = mt(jnp.concatenate([query, query], axis=1), jnp.concatenate([high, rest], axis=1))
        scale = 1.0 / (den_ref[:, lanes] + both[:, PAIR:])
        rden_ref[:, lanes] = scale
        mixed_ref[:, lanes] = ((num_ref[:, lanes] + both[:, :PAIR]) * scale).astype(low)
    resid = x_ref[...].astype(wide) + mm(mixed_ref[...], wo_ref[...])
    resid_ref[...] = resid
    unit, _ = normalised(resid)
    normed = (unit * vec_ref[2:3, :] + vec_ref[3:4, :]).astype(low)
    a_ref[...] = normed
    at_ref[...] = normed.T
    mt_ref[...] = mixed_ref[...].T


def mix(x, vec, wo, fq, num, den, prior, images, span, tokens=()):
    rows_, width = x.shape
    rows = pl.BlockSpec((span, width), lambda b: (b, 0))
    return launch(
        mix_kernel,
        tokens,
        grid=(images,),
        in_specs=[
            rows,
            whole(vec.shape),
            whole(wo.shape),
            rows,
            rows,
            rows,
            pl.BlockSpec((1,) + prior.shape[1:], lambda b: (b, 0, 0, 0)),
        ],
        out_specs=[rows, rows, rows, rows, turned_block(width, span), turned_block(width, span)],
        out_shape=[
            shaped((rows_, width), low),
            shaped((rows_, width), wide),
            shaped((rows_, width), wide),
            shaped((rows_, width), low),
            turned_shape(images, width, span),
            turned_shape(images, width, span),
        ],
        cost_estimate=cost(4 * rows_ * width * width, 24 * rows_ * width + 2 * width * width),
        name="mix",
    )(x, vec, wo, fq, num, den, prior)


gelu_scale = 0.7978845608028654
gelu_cubic = 0.044715


def feed_kernel(fresh, bits, spot_ref, *refs):
    a_ref, e_ref = refs[:2]
    out_ref, da_ref, kept_ref, sent_ref, joined_ref = refs[-5:]
    join(joined_ref, bits, spot_ref, *refs[2:6])

    @pl.when(pl.program_id(0) == 0)
    def _():
        if fresh:
            out_ref[...] = jnp.zeros_like(out_ref)
            da_ref[...] = jnp.zeros_like(da_ref)
        else:
            out_ref[...] = refs[6][...]
            da_ref[...] = refs[7][...]

    up, down = joined_ref[0], joined_ref[1]
    upper = mm(a_ref[...], up)
    grad = mm(e_ref[...], down)
    square = upper * upper
    bend = jnp.tanh(gelu_scale * upper * (1.0 + gelu_cubic * square))
    gate = 0.5 + 0.5 * bend
    hidden = (upper * gate).astype(low)
    slope = gate + 0.5 * upper * (1.0 - bend * bend) * (gelu_scale * (1.0 + 3.0 * gelu_cubic * square))
    dupper = (grad * slope).astype(low)
    out_ref[...] += mt(hidden, down)
    da_ref[...] += mt(dupper, up)
    first = spot_ref[0] == 0
    kept_ref[...] = jnp.where(first, dupper, hidden)
    sent_ref[...] = jnp.where(first, hidden, dupper)


def feed(pieces, a, e, carried, tokens=()):
    rows, width = a.shape
    slabs = pieces.arrays[0].shape[0]
    tiles = SLAB // FEED_TILE
    grads = pl.BlockSpec((rows, FEED_TILE), lambda g, spot: (0, g))
    full = whole((rows, width))
    fresh = carried is None
    return launch_at(
        functools.partial(feed_kernel, fresh, pieces.bits),
        pieces.spot,
        tokens,
        grid=(slabs * tiles,),
        in_specs=[full, full]
        + pieces.blocks(FEED_TILE, lambda g, spot: (g // tiles, 0, g % tiles))
        + ([] if fresh else [full, full]),
        out_specs=[full, full, grads, grads],
        out_shape=[shaped((rows, width), wide)] * 2 + [shaped((rows, slabs * SLAB), low)] * 2,
        scratch_shapes=[pltpu.VMEM((2, width, FEED_TILE), low)],
        cost_estimate=cost(4 * rows * width * slabs * SLAB, 4 * (width + rows) * slabs * SLAB + 20 * rows * width),
        name="feed",
    )(a, e, *pieces.arrays, *(() if fresh else carried))


def weigh_kernel(count, spot_ref, lt_ref, lt_other_ref, x_ref, x_other_ref, kept_ref, sent_ref):
    rows = kept_ref.shape[1]
    for k in range(2):
        places = [pl.ds(pl.multiple_of(spot_ref[k * count + n] * rows, rows), rows) for n in range(count)]
        left, other = (jnp.concatenate([ref[place, :] for place in places], axis=0) for ref in (lt_ref, lt_other_ref))
        product = (mm(left, x_ref[...]) + mm(other, x_other_ref[...])).astype(low)
        (sent_ref if k else kept_ref)[...] = product.reshape(count, rows, -1)


def weigh(chain, lt, lt_other, x, x_other, tokens=()):
    lead, rows, columns = x.shape
    width = lt.shape[0]
    keeps, sends = chain.table()
    count = keeps.shape[0]
    tile = min(FEED_TILE, columns)
    full = whole((width, rows))
    column = pl.BlockSpec((None, rows, tile), lambda n, g, spot: (n, 0, g))
    result = pl.BlockSpec((None, count, width // (2 * count), tile), lambda n, g, spot: (n, 0, 0, g))
    chain.take(
        launch_at(
            functools.partial(weigh_kernel, count),
            jnp.concatenate([keeps, sends]),
            tokens,
            grid=(lead, columns // tile),
            in_specs=[full, full, column, column],
            out_specs=[result, result],
            out_shape=[shaped((lead, count, width // (2 * count), columns), low)] * 2,
            cost_estimate=cost(2 * lead * rows * width * columns, 4 * lead * (rows + width) * columns + 4 * rows * width),
            name="weigh",
        )(lt, lt_other, x, x_other)
    )
    chain.start()
    return chain.sends


def turn_back_kernel(core_ref, x_out_ref, da_ref, resid_ref, e_ref, vec_ref, wo_ref, mixed_ref, rden_ref, fq_ref,
                     out_ref, dres_ref, kept_ref, sent_ref, dn_ref, w_ref, state_ref, sums_ref):
    width = da_ref.shape[1]
    resid = resid_ref[...]
    out_ref[...] = (resid + x_out_ref[...]).astype(low)
    unit, scale = normalised(resid)
    da = da_ref[...]

    @pl.when(pl.program_id(0) == 0)
    def _():
        sums_ref[...] = jnp.zeros_like(sums_ref)

    sums_ref[0:1, :] += jnp.sum(da * unit, axis=0, keepdims=True)
    sums_ref[1:2, :] += jnp.sum(da, axis=0, keepdims=True)
    p = da * vec_ref[2:3, :]
    back = p - jnp.mean(p, axis=-1, keepdims=True) - unit * jnp.mean(p * unit, axis=-1, keepdims=True)
    dres = e_ref[...].astype(wide) + scale * back
    dres_ref[...] = dres
    branch = dres.astype(low)
    left, right = branch[:, : width // 2], branch[:, width // 2 :]
    first = core_ref[0] == 0
    kept_ref[...] = jnp.where(first, left, right)
    sent_ref[...] = jnp.where(first, right, left)
    dmixed = mt(branch, wo_ref[...]).astype(low).astype(wide)
    dnumer = dmixed * rden_ref[...]
    dn_ref[...] = dnumer.astype(low)
    w_ref[...] = (-dnumer * mixed_ref[...].astype(wide)).astype(low)
    for pair in range(width // PAIR):
        lanes = slice(pair * PAIR, (pair + 1) * PAIR)
        query = fq_ref[:, lanes]
        state_ref[0, pair, :HEAD_DIM, :] = fold_state(tm(dn_ref[:, lanes], query))
        total = jnp.sum(fold_state(tm(w_ref[:, lanes], query)), axis=0, keepdims=True)
        state_ref[0, pair, HEAD_DIM:, :] = jnp.broadcast_to(total, (STATE_ROWS - HEAD_DIM, PAIR))


def turn_back(x_out, da, resid, e, vec, wo, mixed, rden, fq, images, span, tokens=()):
    rows_, width = da.shape
    rows = pl.BlockSpec((span, width), lambda b, core: (b, 0))
    state = (images, width // PAIR, STATE_ROWS, PAIR)
    half = pl.BlockSpec((span, width // 2), lambda b, core: (b, 0))
    return launch_at(
        turn_back_kernel,
        core_index(),
        tokens,
        grid=(images,),
        in_specs=[rows, rows, rows, rows, whole(vec.shape), whole(wo.shape), rows, rows, rows],
        out_specs=[rows, rows, half, half, rows, rows] + [pl.BlockSpec((1,) + state[1:], lambda b, core: (b, 0, 0, 0)), whole((8, width))],
        out_shape=[
            shaped((rows_, width), low),
            shaped((rows_, width), wide),
            shaped((rows_, width // 2), low),
            shaped((rows_, width // 2), low),
            shaped((rows_, width), low),
            shaped((rows_, width), low),
            shaped(state, wide),
            shaped((8, width), wide),
        ],
        cost_estimate=cost(5 * rows_ * width * width, 30 * rows_ * width),
        name="turn_back",
    )(x_out, da, resid, e, vec, wo, mixed, rden, fq)


def attend_back_kernel(span, fq_ref, fk_ref, v_ref, dn_ref, w_ref, prior_ref, dq_ref, dfk_ref, dv_ref):
    own = first_head(span)
    own_twice = jnp.concatenate([own, own], axis=1)
    below, above = causal_mask(span, True), causal_mask(span, False)
    one = jnp.ones((span, PAIR), low)
    zero = jnp.zeros((span, PAIR), low)
    zero_twice = jnp.zeros((span, 2 * PAIR), low)
    for pair in range(GROUP // PAIR):
        lanes = slice(pair * PAIR, (pair + 1) * PAIR)
        query, key, value = fq_ref[:, lanes], fk_ref[:, lanes], v_ref[:, lanes]
        grads = jnp.concatenate([dn_ref[:, lanes], w_ref[:, lanes]], axis=1)
        extended = jnp.concatenate([value, one], axis=1)
        folded = prior_ref[0, pair]
        matrix = jnp.concatenate(
            [unfold_state(folded[:HEAD_DIM]), unfold_total(folded[HEAD_DIM : HEAD_DIM + 1])], axis=0
        )
        high, rest = split_low(matrix)
        dfq = mm(jnp.concatenate([grads, grads], axis=1), jnp.concatenate([high, rest], axis=0))
        to_query, to_key, to_value = [], [], []
        for mask, both in ((own, own_twice), (jnp.logical_not(own), jnp.logical_not(own_twice))):
            head_grads = jnp.where(both, grads, zero_twice)
            head_query = jnp.where(mask, query, zero)
            head_key = jnp.where(mask, key, zero)
            to_query.append((mt(head_grads, extended).astype(low) * below, head_key))
            to_key.append((mt(extended, head_grads).astype(low) * above, head_query))
            to_value.append((mt(head_key, query).astype(low) * above, head_grads[:, :PAIR]))
        dfq = dfq + pair_mm(*to_query)
        dq_ref[:, lanes] = (dfq * jnp.minimum(query.astype(wide), 1.0)).astype(low)
        dfk_ref[:, lanes] = pair_mm(*to_key)
        dv_ref[:, lanes] = pair_mm(*to_value)


def attend_back(image, fq, fk, v, dn, w, prior, span, tokens=()):
    width = fq.shape[1]
    block = pl.BlockSpec((span, GROUP), lambda p: (image, p))
    column = pl.BlockSpec((span, GROUP), lambda p: (0, p))
    return launch(
        functools.partial(attend_back_kernel, span),
        tokens,
        grid=(width // GROUP,),
        in_specs=[block] * 5 + [pl.BlockSpec((1, GROUP // PAIR) + prior.shape[2:], lambda p: (image, p, 0, 0))],
        out_specs=[column] * 3,
        out_shape=[shaped((span, width), low), shaped((span, width), wide), shaped((span, width), wide)],
        cost_estimate=cost(32 * span * span * width, 24 * span * width),
        name="attend_back",
    )(fq, fk, v, dn, w, prior)


def finish_kernel(images, span, core_ref, *refs):
    fk_ref, v_ref, later_ref, kept_ref, sent_ref = refs[3 * images :]

    def run(out_ref):
        for image in range(images):
            rows = slice(image * span, (image + 1) * span)
            dq_ref, dfk_ref, dvl_ref = refs[3 * image : 3 * image + 3]
            out_ref[0, rows, :] = dq_ref[...]
            for pair in range(GROUP // PAIR):
                lanes = slice(pair * PAIR, (pair + 1) * PAIR)
                folded = later_ref[image, pair]
                high, rest = split_low(unfold_state(folded[:HEAD_DIM]))
                key, value = fk_ref[rows, lanes], v_ref[rows, lanes]
                dfk = dfk_ref[:, lanes] + folded[HEAD_DIM : HEAD_DIM + 1]
                dfk = dfk + mm(jnp.concatenate([value, value], axis=1), jnp.concatenate([high, rest], axis=0))
                dv = dvl_ref[:, lanes] + mt(
                    jnp.concatenate([key, key], axis=1), jnp.concatenate([high, rest], axis=1)
                )
                out_ref[1, rows, lanes] = (dfk * jnp.minimum(key.astype(wide), 1.0)).astype(low)
                out_ref[2, rows, lanes] = dv.astype(low)

    @pl.when(pl.program_id(0) < pl.num_programs(0) // 2)
    def _():
        run(kept_ref)

    @pl.when(pl.program_id(0) >= pl.num_programs(0) // 2)
    def _():
        run(sent_ref)


def finish(parts, fk, v, later, images, span, tokens=()):
    rows, width = fk.shape
    groups = width // GROUP // 2

    def column(g, core):
        return ((g // groups) ^ core[0]) * groups + g % groups

    block = pl.BlockSpec((rows, GROUP), lambda g, core: (0, column(g, core)))
    part = pl.BlockSpec((span, GROUP), lambda g, core: (0, column(g, core)))
    state = pl.BlockSpec((images, GROUP // PAIR) + later.shape[2:], lambda g, core: (0, column(g, core), 0, 0))
    return launch_at(
        functools.partial(finish_kernel, images, span),
        core_index(),
        tokens,
        grid=(2 * groups,),
        in_specs=[part] * (3 * images) + [block] * 2 + [state],
        out_specs=[
            pl.BlockSpec((3, rows, GROUP), lambda g, core: (0, 0, jnp.minimum(g, groups - 1))),
            pl.BlockSpec((3, rows, GROUP), lambda g, core: (0, 0, jnp.maximum(g - groups, 0))),
        ],
        out_shape=[shaped((3, rows, width // 2), low)] * 2,
        cost_estimate=cost(rows * width * 512, 24 * rows * width),
        name="finish",
    )(*[array for image in parts for array in image], fk, v, later)


def enter_kernel(core_ref, kept_ref, sent_ref, *refs):
    weights = refs[:3]
    x_ref, dres_ref, vec_ref, grad_ref, sums_ref = refs[3:]
    half = x_ref.shape[1] // 2
    da = None
    for k, weight in enumerate(weights):
        for ref, side in ((kept_ref, core_ref[0]), (sent_ref, 1 - core_ref[0])):
            part = mt(ref[k], weight[:, pl.ds(pl.multiple_of(side * half, half), half)])
            da = part if da is None else da + part
    unit, scale = normalised(x_ref[...].astype(wide))
    sums_ref[0:1, :] = jnp.sum(da * unit, axis=0, keepdims=True)
    sums_ref[1:2, :] = jnp.sum(da, axis=0, keepdims=True)
    sums_ref[2:, :] = jnp.zeros_like(sums_ref[2:, :])
    p = da * vec_ref[0:1, :]
    back = p - jnp.mean(p, axis=-1, keepdims=True) - unit * jnp.mean(p * unit, axis=-1, keepdims=True)
    grad_ref[...] = (dres_ref[...] + scale * back).astype(low)


def enter(image, kept, sent, weights, x, dres, vec, span, tokens=()):
    width = x.shape[1]
    rows = pl.BlockSpec((span, width), lambda g, core: (image, 0))
    part = pl.BlockSpec((3, span, width // 2), lambda g, core: (0, image, 0))
    return launch_at(
        enter_kernel,
        core_index(),
        tokens,
        grid=(1,),
        in_specs=[part] * 2 + [whole((width, width))] * 3 + [rows, rows, whole(vec.shape)],
        out_specs=[whole((span, width)), whole((8, width))],
        out_shape=[shaped((span, width), low), shaped((8, width), wide)],
        cost_estimate=cost(3 * span * width * width, 14 * span * width + 6 * width * width),
        name="enter",
    )(kept, sent, *weights, x, dres, vec)


def adam_update(master, moment, second, average, gradient, factor, rate):
    clipped = gradient * factor
    moment = beta_first * moment + (1.0 - beta_first) * clipped
    second = beta_second * second + (1.0 - beta_second) * clipped * clipped
    first_hat = moment / (1.0 - beta_first**STEP)
    second_hat = second / (1.0 - beta_second**STEP)
    master = master - rate * (first_hat / (jnp.sqrt(second_hat) + eps_adam) + weight_decay * master)
    average = average_decay * average + (1.0 - average_decay) * master
    return (master, moment, second, average)


def powers(count):
    return [1 << k for k in range(count.bit_length() - 1)]


def core_index():
    return lax.axis_index("seq") % 2


def pos_index():
    return lax.axis_index("seq") // 2


def pos_bits():
    return (lax.axis_size("seq") // 2).bit_length() - 1


def flip(array, axis, bit):
    return lax.ppermute(array, axis, [(i, i ^ bit) for i in range(lax.axis_size(axis))])


def flip_core(array):
    return flip(array, "seq", 1)


def flip_pos(array, stage):
    bits = pos_bits()
    pairs = [(i, i ^ (2 << (stage if i % 2 == 0 else bits - 1 - stage))) for i in range(lax.axis_size("seq"))]
    return lax.ppermute(array, "seq", pairs)


def own_bit(stage):
    bits = pos_bits()
    return jnp.where(core_index() == 0, pos_index() >> stage, pos_index() >> (bits - 1 - stage)) & 1


def halves(shape, dim):
    index = np.arange(int(np.prod(shape))).reshape(shape)
    return np.stack([index.take(side, axis=dim).ravel() for side in range(2)])


def fold_kernel(chains, spot_ref, *refs):
    ins, outs = refs[: 4 * chains], refs[4 * chains :]
    for k in range(2 * chains):
        value = ins[2 * k][...].astype(wide) + ins[2 * k + 1][...].astype(wide)
        outs[k][...] = value.astype(outs[k].dtype)


def fold(cuts, tokens=()):
    count = cuts[0][2].shape[0]
    steps = max(1, min(2, min(kept.shape[-1] for kept, *_ in cuts) // 256))
    in_specs, out_specs, out_shape, arrays, moved = [], [], [], [], 0
    for k, (kept, came, keeps, sends) in enumerate(cuts):
        lead, _, rows, columns = kept.shape
        block = (lead, 1, rows, columns // steps)
        for side in range(2):
            at = 2 * k * count + side * count
            spec = pl.BlockSpec(block, lambda g, c, spot, at=at: (0, spot[at + g], 0, c))
            in_specs += [spec, spec]
            arrays += [kept, came]
            out_specs.append(pl.BlockSpec(block, lambda g, c, spot: (0, g, 0, c)))
            out_shape.append(shaped((lead, count, rows, columns), low if side else wide))
        moved += 8 * kept.size
    results = launch_at(
        functools.partial(fold_kernel, len(cuts)),
        jnp.concatenate([part for _, _, keeps, sends in cuts for part in (keeps, sends)]),
        tokens,
        grid=(count, steps),
        in_specs=in_specs,
        out_specs=out_specs,
        out_shape=out_shape,
        cost_estimate=cost(1, moved),
        name="fold",
    )(*arrays)
    return [results[2 * k : 2 * k + 2] for k in range(len(cuts))]


class Chain:
    def __init__(self, lead=1):
        self.lead = lead
        self.stage = -1
        self.left = [list(range(pos_bits()))[::-1]] * 2

    def start(self):
        self.came = [flip_pos(self.sends[0], self.stage)]

    def table(self):
        self.stage += 1
        tables = []
        for kind in range(2):
            bit = self.stage if kind == 0 else pos_bits() - 1 - self.stage
            left = self.left[kind]
            tables.append(halves((2,) * len(left), left.index(bit)))
            self.left[kind] = [other for other in left if other != bit]
        table = jnp.where(core_index() == 0, *[jnp.asarray(part, jnp.int32) for part in tables])
        own = own_bit(self.stage)
        return table[own], table[1 - own]

    def cut(self):
        return (self.kept, self.came[0], *self.table())

    def take(self, parts):
        self.kept, self.sends = parts[0], [parts[1]]


def advance(chains, tokens=()):
    parts = fold([chain.cut() for chain in chains], tokens)
    for chain, part in zip(chains, parts):
        chain.take(part)
        chain.start()
    return [array for chain in chains for array in chain.sends]


def last_kernel(ways, pre, pieces, spot_ref, *refs):
    ins, outs = refs[: 2 * pieces], refs[2 * pieces :]
    at = 0
    for k in range(pieces):
        columns = ins[2 * k].shape[-1]
        for j in range(ways):
            place = spot_ref[0] ^ j
            for n in range(pre):
                value = ins[2 * k][n, place].astype(wide) + ins[2 * k + 1][n, place].astype(wide)
                outs[j][n, :, at : at + columns] = value.astype(outs[j].dtype)
        at += columns


class Last:
    def __init__(self, chains, tokens=(), slowly=False):
        slices = lax.axis_size("img")
        ways = 2 if slowly else slices
        self.lead = chains[0].lead
        pre = self.lead * 2 * slices // ways
        arrays = []
        for chain in chains:
            for array in (chain.kept, chain.came[0]):
                arrays.append(array.reshape(pre, ways, -1, array.shape[-1]))
        self.widths = [array.shape[-1] for array in arrays[::2]]
        inside = pl.BlockSpec(memory_space=pltpu.VMEM)
        parts = launch(
            functools.partial(last_kernel, ways, pre, len(chains)),
            tokens,
            in_specs=[pl.BlockSpec(memory_space=pltpu.SMEM)] + [inside] * len(arrays),
            out_specs=[inside] * ways,
            out_shape=[shaped((pre, arrays[0].shape[2], sum(self.widths)), low if j else wide) for j in range(ways)],
            cost_estimate=cost(1, 4 * sum(array.size for array in arrays)),
                name="last",
        )((lax.axis_index("img") % ways).reshape(1), *arrays)
        self.kept, self.sends = parts[0], list(parts[1:])
        self.hops = list(range(1, ways))
        self.left = powers(slices)[1:][::-1] if slowly else []
        self.start()

    def start(self):
        self.came = [flip(array, "img", hop) for array, hop in zip(self.sends, self.hops)]

    def cut(self):
        bit = self.left[-1]
        entries = self.kept.reshape((1, -1) + self.kept.shape[-2:])
        dims = (2 * self.lead,) + (2,) * len(self.left)
        table = jnp.asarray(halves(dims, len(dims) - 1), jnp.int32)
        own = (lax.axis_index("img") // bit) % 2
        self.left = self.left[:-1]
        self.hops = [bit]
        return (entries, self.came[0].reshape(entries.shape), table[own], table[1 - own])

    def take(self, parts):
        self.kept, self.sends = parts[0][0], [parts[1][0]]

    def total(self):
        while self.left:
            advance([self])
        total = self.kept
        for came in self.came:
            total = total + came.astype(wide)
        return total

    def settle(self, stretch, tokens):
        self.came[stretch] = gate(self.came[stretch], tokens)
        return self.came[stretch]

    def squares(self):
        self.sums = self.total()
        return jnp.sum(self.sums * self.sums)

    def finish(self):
        core = core_index()
        total = self.sums.reshape((self.lead, 2) + self.sums.shape[-2:])
        own = lax.dynamic_index_in_dim(total, core, 1, False)
        came = flip_core(lax.dynamic_index_in_dim(total, 1 - core, 1, False))
        first, second = jnp.where(core == 0, own, came), jnp.where(core == 0, came, own)
        at, found = 0, []
        for columns in self.widths:
            found.append((first[..., at : at + columns], second[..., at : at + columns]))
            at += columns
        return found


def slow_hops():
    return [(axis, bit) for axis in ("seq", "img") for bit in powers(lax.axis_size(axis))]


def sum_all(array):
    rounds = [("img", range(1, lax.axis_size("img"))), ("seq", range(2, lax.axis_size("seq"), 2)), ("seq", [1])]
    for axis, hops in rounds:
        came = [flip(array, axis, hop) for hop in hops]
        for other in came:
            array = array + other
    return array


def assemble_kernel(plan, spot_ref, *refs):
    outs = sorted({out for _, _, out, _ in plan})
    count = len(refs) - 1 - len(outs)
    sems = refs[-1]
    copies = []
    for k, (piece, cut, out, where) in enumerate(plan):
        source = refs[piece].at[cut] if cut is not None else refs[piece]
        target = refs[count + out].at[where(spot_ref)]
        copies.append(pltpu.make_async_copy(source, target, sems.at[k]))
    for copy in copies:
        copy.start()
    for copy in copies:
        copy.wait()


def assemble(plan, spots, pieces, shapes, tokens=()):
    anywhere = pl.BlockSpec(memory_space=pl.ANY)
    return launch(
        functools.partial(assemble_kernel, plan),
        tokens,
        in_specs=[pl.BlockSpec(memory_space=pltpu.SMEM)] + [anywhere] * len(pieces),
        out_specs=[pl.BlockSpec(memory_space=pltpu.VMEM)] * len(shapes),
        out_shape=[shaped(shape, low) for shape in shapes],
        scratch_shapes=[pltpu.SemaphoreType.DMA((len(plan),))],
        cost_estimate=cost(1, 2 * sum(2 * piece.size for piece in pieces)),
        name="assemble",
    )(jnp.stack(spots).astype(jnp.int32), *pieces)


def gate_kernel(*refs):
    pass


def gate(arrays, tokens):
    anywhere = pl.BlockSpec(memory_space=pl.ANY)
    return launch(
        gate_kernel,
        tokens,
        in_specs=[anywhere] * len(arrays),
        out_specs=[anywhere] * len(arrays),
        out_shape=[shaped(array.shape, array.dtype) for array in arrays],
        input_output_aliases={k: k for k in range(len(arrays))},
        cost_estimate=cost(1, 1),
        name="gate",
    )(*arrays)


class Gather:
    def __init__(self, own, other):
        self.own, self.other = own, other
        self.stage = 0

    def pair(self):
        came = flip_core(self.other)
        pairs = [jnp.stack([self.own, came], axis=1), jnp.stack([came, self.own], axis=1)]
        return jnp.where(core_index() == 0, *pairs)

    @staticmethod
    def exchange(both, tokens=()):
        if tokens:
            (both,) = gate([both], tokens)
        own, other = jnp.split(both, 2)
        every = slice(None)
        plan = [(0, None, 0, lambda spot: (every, spot[0])), (1, None, 0, lambda spot: (every, 1 - spot[0]))]
        k, rows, columns = own.shape
        found = Gather(None, None)
        found.part = assemble(plan, [core_index()], [own, flip_core(other)], [(k, 2, rows, columns)])[0]
        found.part = found.part.reshape(k, 1, 2 * rows, columns)
        return found

    def start_slices(self, hops=False):
        self.pieces = [self.pair()]
        for j in range(1, lax.axis_size("img")):
            bit = j & -j if hops else j
            self.pieces.append(flip(self.pieces[j - bit], "img", bit))

    def finish_slices(self, tokens=(), groups=1):
        slices = len(self.pieces)
        if tokens:
            self.pieces = self.pieces[:1] + list(gate(self.pieces[1:], tokens))
        every = slice(None)
        k, _, rows, columns = self.pieces[0].shape
        k = k // groups
        plan = [
            (j, slice(n * k, (n + 1) * k), n, lambda spot, j=j: (every, every, spot[0] ^ j))
            for n in range(groups)
            for j in range(slices)
        ]
        shape = (k, 2, slices, rows, columns)
        parts = assemble(plan, [lax.axis_index("img")], self.pieces, [shape] * groups)
        found = []
        for part in parts:
            found.append(Gather(None, None))
            found[-1].part = part.reshape(k, 1, 2 * slices * rows, columns)
        return found

    def start_pos(self, tokens=()):
        if tokens:
            (self.part,) = gate([self.part], tokens)
        self.came = flip_pos(self.part, self.stage)
        self.stage += 1

    def finish_pos(self, tokens=()):
        every = slice(None)
        if tokens:
            (self.came,) = gate([self.came], tokens)
        plan = [
            (0, None, 0, lambda spot: (every, spot[0])),
            (1, None, 0, lambda spot: (every, 1 - spot[0])),
        ]
        shape = self.part.shape[:1] + (2,) + self.part.shape[1:]
        self.part = assemble(plan, [own_bit(self.stage - 1)], [self.part, self.came], [shape])[0]
        self.part = self.part.reshape((shape[0], -1) + shape[3:])
        return [self.part]

    def start_last(self):
        self.start_pos()
        self.turned = flip_core(self.part)

    def finish_last(self, tokens, turned_tokens):
        (self.turned,) = gate([self.turned], turned_tokens)
        (self.came,) = gate([self.came], tokens)
        return Pieces([self.part, self.came, self.turned, flip_core(self.came)])


def narrow_kernel(core_ref, weight_ref, *out_refs):
    first = core_ref[0] == 0
    slabs = out_refs[0].shape[0] // 2
    for k, out_ref in enumerate(out_refs):
        for n in range(slabs):
            columns = slice((k * slabs + n) * SLAB, (k * slabs + n + 1) * SLAB)
            left, right = weight_ref[0, :, columns].astype(low), weight_ref[1, :, columns].astype(low)
            out_ref[n] = jnp.where(first, left, right)
            out_ref[slabs + n] = jnp.where(first, right, left)


def narrow(weight, groups, tokens):
    _, owned, hidden = weight.shape
    slabs = hidden // SLAB // groups
    inside = pl.BlockSpec(memory_space=pltpu.VMEM)
    return launch(
        narrow_kernel,
        tokens,
        in_specs=[pl.BlockSpec(memory_space=pltpu.SMEM), inside],
        out_specs=[inside] * groups,
        out_shape=[shaped((2 * slabs, owned, SLAB), low)] * groups,
        cost_estimate=cost(1, 12 * slabs * groups * owned * SLAB),
        name="narrow",
    )(core_index().reshape(1), weight)


class Passing:
    def __init__(self, own, backward, direct):
        self.backward = backward
        came = flip_core(own.astype(low)).astype(wide)
        self.outside = jnp.where(core_index() == (0 if backward else 1), came, 0.0)
        self.total = own + came
        self.bits = powers(lax.axis_size("seq") // 2)
        if direct:
            both = self.total.astype(low)
            self.came = [flip(both, "seq", 2 * j) for j in range(1, lax.axis_size("seq") // 2)]

    def finish(self, tokens):
        total = self.outside
        for j, came in enumerate(gate(self.came, tokens), 1):
            earlier = (pos_index() ^ j) < pos_index()
            total = total + jnp.where(earlier != self.backward, came.astype(wide), 0.0)
        return total

    def hop(self, tokens):
        bit, *self.bits = self.bits
        (came,) = gate([flip(self.total.astype(low), "seq", 2 * bit)], tokens)
        came = came.astype(wide)
        earlier = (pos_index() ^ bit) < pos_index()
        self.outside = self.outside + jnp.where(earlier != self.backward, came, 0.0)
        self.total = self.total + came
        return self.outside


def body(
    images,
    cotangent,
    attention_weight,
    feedforward_weight,
    norm_vectors,
    attention_moment,
    feedforward_moment,
    norm_moment,
    attention_second,
    feedforward_second,
    norm_second,
    attention_average,
    feedforward_average,
    norm_average,
):
    count, span, width = images.shape
    tokens = count * span
    owned = attention_weight.shape[1]
    slabs = feedforward_weight.shape[2] // SLAB
    stages = pos_bits()
    half = slabs // 2
    every = slice(None)

    x, e = images.reshape(tokens, width), cotangent.reshape(tokens, width)
    low_weights = jnp.pad(attention_weight.astype(low), ((0, 0), (0, 0), (0, 128)))
    vectors = jnp.pad(norm_vectors.astype(low).T, ((0, 0), (width, 124)))
    query_weight, key_weight, value_weight, out_weight = low_weights
    kinds = jnp.stack([key_weight, query_weight]), jnp.stack([value_weight + vectors, out_weight])
    first_core = core_index() == 0
    one = Gather(jnp.where(first_core, *kinds), jnp.where(first_core, *kinds[::-1]))
    one.start_slices(True)
    et = turn(e, count, span)
    (one,) = one.finish_slices([et])
    one.start_pos()
    feeds = narrow(feedforward_weight, 2, [one.part])
    marks = [feeds[0]]
    feeds = [lax.all_gather(part, "img", axis=1, tiled=True) for part in feeds]
    for _ in range(stages - 2):
        one.finish_pos(marks)
        one.start_pos()
    one.finish_pos(marks)
    one.start_last()
    pieces = one.finish_last([one.part], [one.part])
    two = Gather.exchange(feeds[0])
    two.start_pos([one.came])
    vec = pieces.second(slice(width, width + 4)).astype(wide).T
    fk, v, a1, a1t, state, wk, wv = project(x, vec, pieces, count, span, [two.part])
    a1t_other = flip_core(a1t)
    prior = Passing(state, False, False)
    for _ in range(stages - 2):
        two.finish_pos([state])
        two.start_pos()
    two.finish_pos([state])
    two.start_last()
    fq, wq, wo = query(a1, pieces, [prior.outside, two.part])
    marks = [prior.hop([fq]), two.turned, a1t_other]
    num, den = attend(fq, fk, v, count, span, marks)
    while prior.bits:
        prior.hop([num])
    prior = prior.outside
    three = Gather.exchange(feeds[1], [num])
    three.start_pos()
    mixed, rden, resid, a2, a2t, mixed_t = mix(x, vec, wo, fq, num, den, prior, count, span, [three.part])
    a2t, mixed_t = turned_whole(a2t), turned_whole(mixed_t)
    lt = jnp.where(first_core, a2t, et)
    lt_other = flip_core(jnp.where(first_core, et, a2t))
    mixed_t_other = flip_core(mixed_t)
    first_pieces = two.finish_last([resid], [fq])
    marks = [resid]
    for _ in range(stages - 2):
        three.finish_pos(marks)
        three.start_pos()
    three.finish_pos(marks)
    three.start_last()
    marks = [three.part, three.turned]

    early = feed(first_pieces, a2, e, None, marks)
    early_other = flip_core(early[3])
    second_pieces = three.finish_last([early[0]], [early[0]])
    late = feed(second_pieces, a2, e, early[:2], [lt_other, mixed_t_other])
    late_other = flip_core(late[3])
    firsts, seconds, outs, inner = [Chain()], [Chain()], [Chain()], [Chain(3)]
    marks = weigh(firsts[0], lt, lt_other, early[2][None], early_other[None], [late[0]])
    output, dres, branch, branch_send, dn, w, dstate, sums_second = turn_back(
        late[0], late[1], resid, e, vec, wo, mixed, rden, fq, count, span, marks + [late_other]
    )
    later = Passing(dstate, True, False)
    marks = [dstate, later.outside]
    for _ in range(stages - 1):
        marks = marks + advance(firsts, [dstate])
    marks = weigh(seconds[0], lt, lt_other, late[2][None], late_other[None], marks)
    passed = later.hop([seconds[0].kept])
    firsts_last = Last(firsts, [seconds[0].kept])
    parts = [attend_back(0, fq, fk, v, dn, w, prior, span, marks + firsts_last.sends + [passed])]
    branch_other = flip_core(gate([branch_send], [parts[0][0]])[0])
    settled = firsts_last.sends
    marks = weigh(outs[0], mixed_t, mixed_t_other, branch[None], branch_other[None], settled)
    for _ in range(stages - 1):
        marks = marks + advance(seconds, [parts[0][0]])
    for image in range(1, count):
        parts.append(attend_back(image, fq, fk, v, dn, w, prior, span, marks))
    for _ in range(stages - 1):
        marks = advance(outs, [parts[-1][0]])
    marks = marks + seconds[0].came + firsts_last.settle(slice(0, None), [parts[-1][0]])
    while later.bits:
        later.hop([parts[-1][0]])
    later = later.outside
    kept, sent = finish(parts, fk, v, later, count, span, marks)
    local_squares = firsts_last.squares()
    came = flip_core(sent)
    seconds_last = Last(seconds + outs, [kept])
    marks = seconds_last.sends + [firsts_last.sums]
    grads_in = [enter(0, kept, sent, (wq, wk, wv), x, dres, vec, span, marks)]
    marks = seconds_last.settle(slice(0, 2), [grads_in[0][1]])
    marks = weigh(inner[0], a1t, a1t_other, kept, came, marks)
    for image in range(1, count):
        grads_in.append(enter(image, kept, sent, (wq, wk, wv), x, dres, vec, span, marks))
    seconds_last.settle(slice(2, None), [grads_in[-1][1]])
    local_squares = local_squares + seconds_last.squares()
    input_grad = jnp.stack([part[0] for part in grads_in])
    sums = sum(part[1] for part in grads_in)
    vector_grad = jnp.concatenate([sums[:2], sums_second[:2]], axis=0)
    hops = slow_hops()
    for axis, bit in hops[:2]:
        vector_grad = vector_grad + flip(vector_grad, axis, bit)
    marks = [seconds_last.sums, vector_grad]
    for _ in range(stages - 1):
        marks = advance(inner, marks)
    (vector_grad,) = gate([vector_grad], marks)
    for axis, bit in hops[2:]:
        vector_grad = vector_grad + flip(vector_grad, axis, bit)
    device = lax.axis_index("seq") * lax.axis_size("img") + lax.axis_index("img")
    vector_shard = lax.dynamic_slice_in_dim(vector_grad, device * owned, owned, 1)
    inner_last = Last(inner, [seconds_last.sums])
    local_squares = local_squares + jnp.sum(vector_shard * vector_shard)
    local_squares = local_squares + inner_last.squares()
    grad_norm = jnp.sqrt(sum_all(jnp.full((8, 128), local_squares))[0, 0])
    (early_shard,) = firsts_last.finish()
    late_shard, out_shard = seconds_last.finish()
    inner_shard = jnp.concatenate([part for pair in inner_last.finish() for part in pair], axis=2)
    attn_shard = jnp.concatenate([inner_shard, jnp.concatenate(out_shard, axis=2)], axis=0)
    feed_shard = jnp.concatenate([jnp.concatenate(pair, axis=2) for pair in zip(early_shard, late_shard)], axis=0)
    factor = clip_bound / jnp.maximum(grad_norm, clip_bound)
    attn_new = adam_update(
        attention_weight, attention_moment, attention_second, attention_average, attn_shard, factor, learn_rate
    )
    feed_new = adam_update(
        feedforward_weight, feedforward_moment, feedforward_second, feedforward_average, feed_shard, factor, learn_rate
    )
    norm_new = adam_update(norm_vectors, norm_moment, norm_second, norm_average, vector_shard, factor, norm_rate)
    output = output.reshape(images.shape)
    input_grad = input_grad.reshape(images.shape)
    return (output, input_grad, grad_norm) + attn_new + feed_new + norm_new


def solution(mesh):
    tokens = P("img", "seq", None)
    rows = P(None, ("seq", "img"), None)
    vectors = P(None, ("seq", "img"))
    group = (rows, rows, vectors)
    return jax.shard_map(
        body,
        mesh=mesh,
        in_specs=(tokens, tokens) + group * 4,
        out_specs=(tokens, tokens, P()) + (rows,) * 8 + (vectors,) * 4,
        check_vma=False,
    )
```

profile of v0, /device:TPU:0, one launch (start us, length us, event | category | flops | bytes accessed | tf_op | source)
XLA Modules:
  0.0 513.2 jit_solution(7459477678966991815)
XLA Ops:
  10.8 4.0 collective-permute-start.2
  16.4 12.2 %collective-permute-done.2.refs_1_ = bf16[2,2,32,1152]{3,2,1,0:T(8,128)(2,1)S(1)} collective-permute-done((bf16[2,2,32,1152]{3,2,1,0:T(8,128)(2,1)S(1)}, bf16[2,2,32,1152]{3,2,1,0:T(8,128)(2,1)S(1)}, u32[]{:S(2)}, u32[]{:S(2)}) %collective-permute-start.2) | collective-permute-done | bytes 294944 | tf_op jit(solution)/shard_map/ppermute | solution.py:720
  29.2 2.5 turn.1.refs_3_
  31.7 5.3 %collective-permute-done.3.refs_2_ = bf16[2,2,32,1152]{3,2,1,0:T(8,128)(2,1)S(1)} collective-permute-done((bf16[2,2,32,1152]{3,2,1,0:T(8,128)(2,1)S(1)}, bf16[2,2,32,1152]{3,2,1,0:T(8,128)(2,1)S(1)}, u32[]{:S(2)}, u32[]{:S(2)}) %collective-permute-start.3) | collective-permute-done | bytes 294944 | tf_op jit(solution)/shard_map/ppermute | solution.py:720
  37.8 2.3 assemble.6
  41.3 2.0 narrow.1
  43.4 13.1 %collective-permute-done.4.refs_0_ = bf16[2,1,256,1152]{3,2,1,0:T(8,128)(2,1)S(1)} collective-permute-done((bf16[2,1,256,1152]{3,2,1,0:T(8,128)(2,1)}, bf16[2,1,256,1152]{3,2,1,0:T(8,128)(2,1)S(1)}, u32[]{:S(2)}, u32[]{:S(2)}) %collective-permute-start.4) | collective-permute-done | bytes 1179680 | tf_op jit(solution)/shard_map/ppermute | solution.py:730
  57.6 3.1 assemble.7
  62.1 27.6 %collective-permute-done.6.refs_0_ = bf16[2,2,256,1152]{3,2,1,0:T(8,128)(2,1)S(1)} collective-permute-done((bf16[2,2,256,1152]{3,2,1,0:T(8,128)(2,1)}, bf16[2,2,256,1152]{3,2,1,0:T(8,128)(2,1)S(1)}, u32[]{:S(2)}, u32[]{:S(2)}) %collective-permute-start.6) | collective-permute-done | bytes 2359328 | tf_op jit(solution)/shard_map/ppermute | solution.py:730
  91.2 2.1 fusion.26
  93.7 2.7 collective-permute-done.8.refs_2_
  97.3 2.2 assemble.8
  104.4 11.3 %project.1 = (bf16[768,1024]{1,0:T(8,128)(2,1)}, bf16[768,1024]{1,0:T(8,128)(2,1)}, bf16[768,1024]{1,0:T(8,128)(2,1)}, bf16[1024,768]{1,0:T(8,128)(2,1)}, f32[2,...) custom-call(s32[3]{0:T(128)} %pad_add_fusion.spot_ref, bf16[768,1024]{1,0:T(8,128)(2,1)} %bitcast.92, ...), custom_call_target="tpu_custom_call" | custom-call | flops 3221225472 | bytes 17825792 | tf_op jit(solution)/shard_map/project/pallas_call | solution.py:73
  116.7 2.9 assemble.9
  120.4 4.4 collective-permute-done.9
  127.9 7.7 %query.1 = (bf16[768,1024]{1,0:T(8,128)(2,1)}, bf16[1024,1024]{1,0:T(8,128)(2,1)}, bf16[1024,1024]{1,0:T(8,128)(2,1)}) custom-call(s32[3]{0:T(128)} %pad_add_fusion.spot_ref, bf16[768,1024]{1,0:T(8,128)(2,1)} %get-tuple-element.103.refs_0_, bf16[2,512,1152]{2,1,0:T(8,128)(2,1)} %bitcast.87, bf16[2,512,1152]{2,1,0:T(8,128)(2,1)} %bitcast.90, ...), custom_call_target="tpu_custom_call" | custom-call | flops 1610612736 | bytes 9437184 | tf_op jit(solution)/shard_map/query/pallas_call | solution.py:73
  137.3 2.1 fusion.2
  139.4 11.1 %attend.1 = (f32[768,1024]{1,0:T(8,128)}, f32[768,1024]{1,0:T(8,128)}) custom-call(bf16[768,1024]{1,0:T(8,128)(2,1)} %get-tuple-element.106.refs_1_.refs_0_.refs_3_.refs_8_, bf16[768,1024]{1,0:T(8,128)(2,1)} %get-tuple-element.107.refs_1_.refs_6_, bf16[768,1024]{1,0:T(8,128)(2,1)} %get-tuple-element.108.refs_2_.refs_7_, ...), custom_call_target="tpu_custom_call" | custom-call | flops 9663676416 | bytes 11010048 | tf_op jit(solution)/shard_map/attend/pallas_call | solution.py:52
  150.5 2.1 fusion.25
  155.4 2.2 assemble.10
  158.7 4.5 collective-permute-done.14.refs_0_
  163.9 1.9 select_add_fusion.1.refs_6_.refs_5_
  165.8 9.9 %mix.1 = (bf16[768,1024]{1,0:T(8,128)(2,1)}, f32[768,1024]{1,0:T(8,128)}, f32[768,1024]{1,0:T(8,128)}, bf16[768,1024]{1,0:T(8,128)(2,1)}, bf16[1024,768]{1,0:T(8,128)(2,1)}, /*index=5*/bf16[1024,768]{1,0:T(8,128)(2,1)}) custom-call(bf16[768,1024]{1,0:T(8,128)(2,1)} %bitcast.93, f32[4,1024]{1,0:T(4,128)} %bitcast.134, ...), custom_call_target="tpu_custom_call" | custom-call | flops 6442450944 | bytes 20971520 | tf_op jit(solution)/shard_map/mix/pallas_call | solution.py:52
  175.9 2.9 assemble.11
  180.9 2.4 collective-permute-done.20.refs_7_.refs_0_
  184.7 21.5 %feed.2 = (f32[768,1024]{1,0:T(8,128)}, f32[768,1024]{1,0:T(8,128)}, bf16[768,2048]{1,0:T(8,128)(2,1)}, bf16[768,2048]{1,0:T(8,128)(2,1)}) custom-call(s32[3]{0:T(128)} %pad_add_fusion.spot_ref, bf16[768,1024]{1,0:T(8,128)(2,1)} %get-tuple-element.113.refs_0_, bf16[768,1024]{1,0:T(8,128)(2,1)} %bitcast.119, bf16[2,512,1024]{2,1,0:T(8,128)(2,1)} %bitcast.104, ...), custom_call_target="tpu_custom_call" | custom-call | flops 12884901888 | bytes 30408704 | tf_op jit(solution)/shard_map/feed/pallas_call | solution.py:73
  211.7 3.5 collective-permute-done.22.refs_8_.refs_1_
  217.8 22.9 %feed.3 = (f32[768,1024]{1,0:T(8,128)}, f32[768,1024]{1,0:T(8,128)}, bf16[768,2048]{1,0:T(8,128)(2,1)}, bf16[768,2048]{1,0:T(8,128)(2,1)}) custom-call(s32[3]{0:T(128)} %pad_add_fusion.spot_ref, bf16[768,1024]{1,0:T(8,128)(2,1)} %get-tuple-element.113.refs_0_, bf16[768,1024]{1,0:T(8,128)(2,1)} %bitcast.120, bf16[2,512,1024]{2,1,0:T(8,128)(2,1)} %bitcast.116, ...), custom_call_target="tpu_custom_call" | custom-call | flops 12884901888 | bytes 30408704 | tf_op jit(solution)/shard_map/feed/pallas_call | solution.py:73
  243.4 11.4 %weigh.4 = (bf16[1,2,256,2048]{3,2,1,0:T(8,128)(2,1)}, bf16[1,2,256,2048]{3,2,1,0:T(8,128)(2,1)}) custom-call(s32[4]{0:T(128)} %pad_add_fusion.1.spot_ref, bf16[1024,768]{1,0:T(8,128)(2,1)} %get-tuple-element.203.refs_0_, bf16[1024,768]{1,0:T(8,128)(2,1)} %copy-done.71, bf16[1,768,2048]{2,1,0:T(8,128)(2,1)} %bitcast.144, bf16[1,768,2048]{2,1,0:T(8,128)(2,1)} %bitcast.140, ...), custom_call_target="tpu_custom_call" | custom-call | flops 6442450944 | bytes 17825792 | tf_op jit(solution)/shard_map/weigh/pallas_call | solution.py:73
  255.8 12.9 %turn_back.1 = (bf16[768,1024]{1,0:T(8,128)(2,1)}, f32[768,1024]{1,0:T(8,128)}, bf16[768,512]{1,0:T(8,128)(2,1)}, bf16[768,512]{1,0:T(8,128)(2,1)}, bf16[768,102...) custom-call(s32[1]{0:T(128)} %bitcast.refs_0_.spot_ref, ...), custom_call_target="tpu_custom_call" | custom-call | flops 8053063680 | bytes 23592960 | tf_op jit(solution)/shard_map/turn_back/pallas_call | solution.py:73
  270.9 1.9 pad_add_fusion.2.spot_ref
  272.8 8.3 %collective-permute-done.27.refs_1_.refs_3_ = bf16[1,2,256,2048]{3,2,1,0:T(8,128)(2,1)S(1)} collective-permute-done((bf16[1,2,256,2048]{3,2,1,0:T(8,128)(2,1)}, bf16[1,2,256,2048]{3,2,1,0:T(8,128)(2,1)S(1)}, u32[]{:S(2)}, u32[]{:S(2)}) %collective-permute-start.27) | collective-permute-done | bytes 2097184 | tf_op jit(solution)/shard_map/ppermute | solution.py:730
  282.4 4.3 fold.4
  289.7 11.6 %weigh.5 = (bf16[1,2,256,2048]{3,2,1,0:T(8,128)(2,1)}, bf16[1,2,256,2048]{3,2,1,0:T(8,128)(2,1)}) custom-call(s32[4]{0:T(128)} %pad_add_fusion.1.spot_ref, bf16[1024,768]{1,0:T(8,128)(2,1)} %get-tuple-element.203.refs_0_, bf16[1024,768]{1,0:T(8,128)(2,1)} %copy-done.71, bf16[1,768,2048]{2,1,0:T(8,128)(2,1)} %bitcast.143, ...), custom_call_target="tpu_custom_call" | custom-call | flops 6442450944 | bytes 17825792 | tf_op jit(solution)/shard_map/weigh/pallas_call | solution.py:73
  303.6 2.0 fusion.4
  306.5 3.1 last.3
  309.6 12.0 %attend_back.2 = (bf16[384,1024]{1,0:T(8,128)(2,1)}, f32[384,1024]{1,0:T(8,128)}, f32[384,1024]{1,0:T(8,128)}) custom-call(bf16[768,1024]{1,0:T(8,128)(2,1)} %get-tuple-element.106.refs_1_.refs_0_.refs_3_.refs_8_, bf16[768,1024]{1,0:T(8,128)(2,1)} %get-tuple-element.107.refs_1_.refs_6_, bf16[768,1024]{1,0:T(8,128)(2,1)} %get-tuple-element.108.refs_2_.refs_7_, ...), custom_call_target="tpu_custom_call" | custom-call | flops 9663676416 | bytes 9437184 | tf_op jit(solution)/shard_map/attend_back/pallas_call | solution.py:52
  321.6 6.2 %collective-permute-start.30 = (bf16[768,512]{1,0:T(8,128)(2,1)}, bf16[768,512]{1,0:T(8,128)(2,1)S(1)}, u32[]{:S(2)}, u32[]{:S(2)}) collective-permute-start(bf16[768,512]{1,0:T(8,128)(2,1)} %gate.36), channel_id=1, source_target_pairs={{0,4},{4,0},{8,12},{12,8},{16,20},{20,16},{24,28},{28,24},{1,5},{5... | collective-permute-start | bytes 2359304 | tf_op jit(solution)/shard_map/ppermute | solution.py:720
  327.9 2.1 collective-permute-start.32
  331.4 3.4 collective-permute-start.36
  335.6 5.6 %weigh.6 = (bf16[1,2,256,512]{3,2,1,0:T(8,128)(2,1)}, bf16[1,2,256,512]{3,2,1,0:T(8,128)(2,1)}) custom-call(s32[4]{0:T(128)} %pad_add_fusion.1.spot_ref, bf16[1024,768]{1,0:T(8,128)(2,1)} %get-tuple-element.118.refs_0_, bf16[1024,768]{1,0:T(8,128)(2,1)} %copy-done.70, bf16[1,768,512]{2,1,0:T(8,128)(2,1)} %bitcast.146, bf16[1,768,512]{2,1,0:T(8,128)(2,1)} %bitcast.142, ...), custom_call_target="tpu_custom_call" | custom-call | flops 1610612736 | bytes 6815744 | tf_op jit(solution)/shard_map/weigh/pallas_call | solution.py:73
  342.6 4.1 fold.5
  347.5 12.1 %attend_back.3 = (bf16[384,1024]{1,0:T(8,128)(2,1)}, f32[384,1024]{1,0:T(8,128)}, f32[384,1024]{1,0:T(8,128)}) custom-call(bf16[768,1024]{1,0:T(8,128)(2,1)} %get-tuple-element.106.refs_1_.refs_0_.refs_3_.refs_8_, bf16[768,1024]{1,0:T(8,128)(2,1)} %get-tuple-element.107.refs_1_.refs_6_, bf16[768,1024]{1,0:T(8,128)(2,1)} %get-tuple-element.108.refs_2_.refs_7_, ...), custom_call_target="tpu_custom_call" | custom-call | flops 9663676416 | bytes 9437184 | tf_op jit(solution)/shard_map/attend_back/pallas_call | solution.py:52
  360.4 2.9 fold.6
  366.7 8.1 %finish.1 = (bf16[3,768,512]{2,1,0:T(8,128)(2,1)}, bf16[3,768,512]{2,1,0:T(8,128)(2,1)}) custom-call(s32[1]{0:T(128)} %bitcast.refs_0_.spot_ref, bf16[384,1024]{1,0:T(8,128)(2,1)} %get-tuple-element.140.refs_1_.refs_4_.refs_0_, f32[384,1024]{1,0:T(8,128)} %get-tuple-element.141.refs_1_, f32[384,1024]{1,0:T(8,128)} %get-tuple-element.142.refs_2_, ...), custom_call_target="tpu_custom_call" | custom-call | flops 805306368 | bytes 18874368 | tf_op jit(solution)/shard_map/finish/pallas_call | solution.py:73
  376.3 5.1 collective-permute-done.38
  382.0 3.5 last.4
  385.5 2.8 collective-permute-start.41
  389.9 8.4 %enter.2 = (bf16[384,1024]{1,0:T(8,128)(2,1)}, f32[8,1024]{1,0:T(8,128)}) custom-call(s32[1]{0:T(128)} %bitcast.refs_0_.spot_ref, bf16[3,768,512]{2,1,0:T(8,128)(2,1)} %get-tuple-element.155.refs_5_.refs_0_.refs_2_, bf16[3,768,512]{2,1,0:T(8,128)(2,1)} %get-tuple-element.156.refs_1_, bf16[1024,1024]{1,0:T(8,128)(2,1)} %get-tuple-element.157.refs_2_, ...), custom_call_target="tpu_custom_call" | custom-call | flops 2415919104 | bytes 11796480 | tf_op jit(solution)/shard_map/enter/pallas_call | solution.py:73
  398.3 3.3 collective-permute-done.40.refs_0_
  405.1 9.4 %weigh.7 = (bf16[3,2,256,512]{3,2,1,0:T(8,128)(2,1)}, bf16[3,2,256,512]{3,2,1,0:T(8,128)(2,1)}) custom-call(s32[4]{0:T(128)} %pad_add_fusion.1.spot_ref, bf16[1024,768]{1,0:T(8,128)(2,1)} %get-tuple-element.109.refs_0_, bf16[1024,768]{1,0:T(8,128)(2,1)} %collective-permute-done.13.refs_5_.refs_1_, ...), custom_call_target="tpu_custom_call" | custom-call | flops 4831838208 | bytes 14155776 | tf_op jit(solution)/shard_map/weigh/pallas_call | solution.py:73
  415.9 2.4 collective-permute-start.42
  418.2 8.4 %enter.3 = (bf16[384,1024]{1,0:T(8,128)(2,1)}, f32[8,1024]{1,0:T(8,128)}) custom-call(s32[1]{0:T(128)} %bitcast.refs_0_.spot_ref, bf16[3,768,512]{2,1,0:T(8,128)(2,1)} %get-tuple-element.155.refs_5_.refs_0_.refs_2_, bf16[3,768,512]{2,1,0:T(8,128)(2,1)} %get-tuple-element.156.refs_1_, bf16[1024,1024]{1,0:T(8,128)(2,1)} %get-tuple-element.157.refs_2_, ...), custom_call_target="tpu_custom_call" | custom-call | flops 2415919104 | bytes 11796480 | tf_op jit(solution)/shard_map/enter/pallas_call | solution.py:73
  431.8 2.6 multiply_reduce_fusion
  437.3 4.1 fold.7
  441.4 2.0 collective-permute-start.49
  443.7 10.3 %collective-permute-done.46 = f32[4,1024]{1,0:T(4,128)S(1)} collective-permute-done((f32[4,1024]{1,0:T(4,128)}, f32[4,1024]{1,0:T(4,128)S(1)}, u32[]{:S(2)}, u32[]{:S(2)}) %collective-permute-start.46) | collective-permute-done | bytes 16416 | tf_op jit(solution)/shard_map/ppermute | solution.py:720
  454.7 2.6 collective-permute-start.47
  461.9 2.8 last.5
  465.1 2.6 collective-permute-start.51
  472.4 3.8 collective-permute-done.51
  476.9 1.8 multiply_reduce_fusion.2
  479.3 2.7 collective-permute-start.53
  497.1 4.4 multiply_add_fusion
  (327 shorter events, 105.8 us)
Async XLA Ops:
  7.2 84.0 %all-gather.3.cloned.1.call-start = ((), (), s32[]{:S(2)}) async-start(), calls=%async_computation | async-start | bytes 1310720 | tf_op jit(solution)/shard_map/all_gather | solution.py:1128
  9.2 1.5 collective-permute-start
  10.8 17.8 %collective-permute-start.2 = (bf16[2,2,32,1152]{3,2,1,0:T(8,128)(2,1)S(1)}, bf16[2,2,32,1152]{3,2,1,0:T(8,128)(2,1)S(1)}, u32[]{:S(2)}, u32[]{:S(2)}) collective-permute-start(bf16[2,2,32,1152]{3,2,1,0:T(8,128)(2,1)S(1)} %maximum_select_fusion.refs_1_), channel_id=1, source_target_pairs={{0,2},{1,3},{2,0},{3,1},{4,6},{5,7},{6,4},{7,5},{8,10},{9,11},{10,... | collective-permute-start | bytes 884744 | tf_op jit(solution)/shard_map/ppermute | solution.py:720
  14.8 16.9 %collective-permute-start.1 = (bf16[2,2,32,1152]{3,2,1,0:T(8,128)(2,1)S(1)}, bf16[2,2,32,1152]{3,2,1,0:T(8,128)(2,1)S(1)}, u32[]{:S(2)}, u32[]{:S(2)}) collective-permute-start(bf16[2,2,32,1152]{3,2,1,0:T(8,128)(2,1)S(1)} %maximum_select_fusion.refs_1_), channel_id=1, source_target_pairs={{0,1},{1,0},{2,3},{3,2},{4,5},{5,4},{6,7},{7,6},{8,9},{9,8},{10,11... | collective-permute-start | bytes 884744 | tf_op jit(solution)/shard_map/ppermute | solution.py:720
  28.6 8.5 %collective-permute-start.3 = (bf16[2,2,32,1152]{3,2,1,0:T(8,128)(2,1)S(1)}, bf16[2,2,32,1152]{3,2,1,0:T(8,128)(2,1)S(1)}, u32[]{:S(2)}, u32[]{:S(2)}) collective-permute-start(bf16[2,2,32,1152]{3,2,1,0:T(8,128)(2,1)S(1)} %collective-permute-done.2.refs_1_), channel_id=1, source_target_pairs={{0,1},{1,0},{2,3},{3,2},{4,5},{5,4},{6,7},{7,6},{8,9},{9,8},{10,11... | collective-permute-start | bytes 884744 | tf_op jit(solution)/shard_map/ppermute | solution.py:720
  40.1 16.5 %collective-permute-start.4 = (bf16[2,1,256,1152]{3,2,1,0:T(8,128)(2,1)}, bf16[2,1,256,1152]{3,2,1,0:T(8,128)(2,1)S(1)}, u32[]{:S(2)}, u32[]{:S(2)}) collective-permute-start(bf16[2,1,256,1152]{3,2,1,0:T(8,128)(2,1)} %bitcast.96), channel_id=1, source_target_pairs={{0,8},{4,20},{8,0},{12,28},{16,24},{20,4},{24,16},{28,12},{1,9},{5... | collective-permute-start | bytes 3538952 | tf_op jit(solution)/shard_map/ppermute | solution.py:730
  60.7 29.1 %collective-permute-start.6 = (bf16[2,2,256,1152]{3,2,1,0:T(8,128)(2,1)}, bf16[2,2,256,1152]{3,2,1,0:T(8,128)(2,1)S(1)}, u32[]{:S(2)}, u32[]{:S(2)}) collective-permute-start(bf16[2,2,256,1152]{3,2,1,0:T(8,128)(2,1)} %bitcast.81), channel_id=1, source_target_pairs={{0,16},{4,12},{8,24},{12,4},{16,0},{20,28},{24,8},{28,20},{1,17},{... | collective-permute-start | bytes 7077896 | tf_op jit(solution)/shard_map/ppermute | solution.py:730
  62.0 88.5 %all-gather.5.cloned.1.call-start = ((), (), s32[]{:S(2)}) async-start(), calls=%async_computation.1 | async-start | bytes 1310720 | tf_op jit(solution)/shard_map/all_gather | solution.py:1128
  62.1 39.3 %collective-permute-start.5 = (bf16[2,2,256,1152]{3,2,1,0:T(8,128)(2,1)}, bf16[2,2,256,1152]{3,2,1,0:T(8,128)(2,1)}, u32[]{:S(2)}, u32[]{:S(2)}) collective-permute-start(bf16[2,2,256,1152]{3,2,1,0:T(8,128)(2,1)} %bitcast.82), channel_id=1, source_target_pairs={{0,4},{4,0},{8,12},{12,8},{16,20},{20,16},{24,28},{28,24},{1,5},{5... | collective-permute-start | bytes 7077896 | tf_op jit(solution)/shard_map/ppermute | solution.py:720
  91.2 11.3 %collective-permute-start.7 = (bf16[2,2,256,1152]{3,2,1,0:T(8,128)(2,1)}, bf16[2,2,256,1152]{3,2,1,0:T(8,128)(2,1)S(1)}, u32[]{:S(2)}, u32[]{:S(2)}) collective-permute-start(bf16[2,2,256,1152]{3,2,1,0:T(8,128)(2,1)} %gate.24.refs_1_), channel_id=1, source_target_pairs={{0,4},{4,0},{8,12},{12,8},{16,20},{20,16},{24,28},{28,24},{1,5},{5... | collective-permute-start | bytes 7077896 | tf_op jit(solution)/shard_map/ppermute | solution.py:720
  93.2 3.2 collective-permute-start.8
  99.5 16.3 %collective-permute-start.10 = (bf16[2,1,256,1024]{3,2,1,0:T(8,128)(2,1)}, bf16[2,1,256,1024]{3,2,1,0:T(8,128)(2,1)S(1)}, u32[]{:S(2)}, u32[]{:S(2)}) collective-permute-start(bf16[2,1,256,1024]{3,2,1,0:T(8,128)(2,1)} %gate.25.refs_6_.refs_1_), channel_id=1, source_target_pairs={{0,8},{4,20},{8,0},{12,28},{16,24},{20,4},{24,16},{28,12},{1,9},{5... | collective-permute-start | bytes 3145736 | tf_op jit(solution)/shard_map/ppermute | solution.py:730
  119.6 19.8 %collective-permute-start.12 = (bf16[2,2,256,1024]{3,2,1,0:T(8,128)(2,1)}, bf16[2,2,256,1024]{3,2,1,0:T(8,128)(2,1)}, u32[]{:S(2)}, u32[]{:S(2)}) collective-permute-start(bf16[2,2,256,1024]{3,2,1,0:T(8,128)(2,1)} %bitcast.102), channel_id=1, source_target_pairs={{0,4},{4,0},{8,12},{12,8},{16,20},{20,16},{24,28},{28,24},{1,5},{5... | collective-permute-start | bytes 6291464 | tf_op jit(solution)/shard_map/ppermute | solution.py:720
  119.7 19.7 %collective-permute-start.13 = (bf16[1024,768]{1,0:T(8,128)(2,1)}, bf16[1024,768]{1,0:T(8,128)(2,1)}, u32[]{:S(2)}, u32[]{:S(2)}) collective-permute-start(bf16[1024,768]{1,0:T(8,128)(2,1)} %get-tuple-element.109.refs_0_), channel_id=1, source_target_pairs={{0,4},{4,0},{8,12},{12,8},{16,20},{20,16},{24,28},{28,24},{1,5},{5... | collective-permute-start | bytes 4718600 | tf_op jit(solution)/shard_map/ppermute | solution.py:720
  120.3 4.5 collective-permute-start.9
  125.8 10.8 %collective-permute-start.11 = (bf16[2,8,80,128]{3,2,1,0:T(8,128)(2,1)}, bf16[2,8,80,128]{3,2,1,0:T(8,128)(2,1)S(1)}, u32[]{:S(2)}, u32[]{:S(2)}) collective-permute-start(bf16[2,8,80,128]{3,2,1,0:T(8,128)(2,1)} %get-tuple-element.221), channel_id=1, source_target_pairs={{0,8},{4,12},{8,0},{12,4},{16,24},{20,28},{24,16},{28,20},{1,9},{5... | collective-permute-start | bytes 983048 | tf_op jit(solution)/shard_map/ppermute | solution.py:720
  126.9 48.9 %collective-permute-start.18 = (bf16[2,2,256,1024]{3,2,1,0:T(8,128)(2,1)S(1)}, bf16[2,2,256,1024]{3,2,1,0:T(8,128)(2,1)}, u32[]{:S(2)}, u32[]{:S(2)}) collective-permute-start(bf16[2,2,256,1024]{3,2,1,0:T(8,128)(2,1)S(1)} %bitcast.105), channel_id=1, source_target_pairs={{0,16},{4,12},{8,24},{12,4},{16,0},{20,28},{24,8},{28,20},{1,17},{... | collective-permute-start | bytes 6291464 | tf_op jit(solution)/shard_map/ppermute | solution.py:730
  152.7 1.9 collective-permute-start.15
  152.7 10.5 %collective-permute-start.14 = (bf16[2,8,80,128]{3,2,1,0:T(8,128)(2,1)S(1)}, bf16[2,8,80,128]{3,2,1,0:T(8,128)(2,1)S(1)}, u32[]{:S(2)}, u32[]{:S(2)}) collective-permute-start(bf16[2,8,80,128]{3,2,1,0:T(8,128)(2,1)S(1)} %copy-done.55), channel_id=1, source_target_pairs={{0,16},{4,20},{8,24},{12,28},{16,0},{20,4},{24,8},{28,12},{1,17},{... | collective-permute-start | bytes 983048 | tf_op jit(solution)/shard_map/ppermute | solution.py:720
  157.6 18.2 %collective-permute-start.16 = (bf16[2,1,256,1024]{3,2,1,0:T(8,128)(2,1)}, bf16[2,1,256,1024]{3,2,1,0:T(8,128)(2,1)}, u32[]{:S(2)}, u32[]{:S(2)}) collective-permute-start(bf16[2,1,256,1024]{3,2,1,0:T(8,128)(2,1)} %bitcast.106), channel_id=1, source_target_pairs={{0,8},{4,20},{8,0},{12,28},{16,24},{20,4},{24,16},{28,12},{1,9},{5... | collective-permute-start | bytes 3145736 | tf_op jit(solution)/shard_map/ppermute | solution.py:730
  175.8 5.1 collective-permute-start.19
  178.8 4.6 collective-permute-start.20
  179.3 26.9 %collective-permute-start.17 = (bf16[2,2,256,1024]{3,2,1,0:T(8,128)(2,1)}, bf16[2,2,256,1024]{3,2,1,0:T(8,128)(2,1)S(1)}, u32[]{:S(2)}, u32[]{:S(2)}) collective-permute-start(bf16[2,2,256,1024]{3,2,1,0:T(8,128)(2,1)} %bitcast.114), channel_id=1, source_target_pairs={{0,16},{4,12},{8,24},{12,4},{16,0},{20,28},{24,8},{28,20},{1,17},{... | collective-permute-start | bytes 6291464 | tf_op jit(solution)/shard_map/ppermute | solution.py:730
  207.6 9.1 %collective-permute-start.21 = (bf16[2,2,256,1024]{3,2,1,0:T(8,128)(2,1)}, bf16[2,2,256,1024]{3,2,1,0:T(8,128)(2,1)}, u32[]{:S(2)}, u32[]{:S(2)}) collective-permute-start(bf16[2,2,256,1024]{3,2,1,0:T(8,128)(2,1)} %gate.33), channel_id=1, source_target_pairs={{0,4},{4,0},{8,12},{12,8},{16,20},{20,16},{24,28},{28,24},{1,5},{5... | collective-permute-start | bytes 6291464 | tf_op jit(solution)/shard_map/ppermute | solution.py:720
  210.8 4.4 collective-permute-start.22
  211.2 5.5 %collective-permute-start.23 = (bf16[1024,768]{1,0:T(8,128)(2,1)}, bf16[1024,768]{1,0:T(8,128)(2,1)S(1)}, u32[]{:S(2)}, u32[]{:S(2)}) collective-permute-start(bf16[1024,768]{1,0:T(8,128)(2,1)} %get-tuple-element.118.refs_0_), channel_id=1, source_target_pairs={{0,4},{4,0},{8,12},{12,8},{16,20},{20,16},{24,28},{28,24},{1,5},{5... | collective-permute-start | bytes 4718600 | tf_op jit(solution)/shard_map/ppermute | solution.py:720
  211.3 30.5 %collective-permute-start.24 = (bf16[768,2048]{1,0:T(8,128)(2,1)}, bf16[768,2048]{1,0:T(8,128)(2,1)S(1)}, u32[]{:S(2)}, u32[]{:S(2)}) collective-permute-start(bf16[768,2048]{1,0:T(8,128)(2,1)} %get-tuple-element.124), channel_id=1, source_target_pairs={{0,4},{4,0},{8,12},{12,8},{16,20},{20,16},{24,28},{28,24},{1,5},{5... | collective-permute-start | bytes 9437192 | tf_op jit(solution)/shard_map/ppermute | solution.py:720
  240.7 15.1 %collective-permute-start.25 = (bf16[768,2048]{1,0:T(8,128)(2,1)}, bf16[768,2048]{1,0:T(8,128)(2,1)}, u32[]{:S(2)}, u32[]{:S(2)}) collective-permute-start(bf16[768,2048]{1,0:T(8,128)(2,1)} %get-tuple-element.126), channel_id=1, source_target_pairs={{0,4},{4,0},{8,12},{12,8},{16,20},{20,16},{24,28},{28,24},{1,5},{5... | collective-permute-start | bytes 9437192 | tf_op jit(solution)/shard_map/ppermute | solution.py:720
  254.9 26.2 %collective-permute-start.27 = (bf16[1,2,256,2048]{3,2,1,0:T(8,128)(2,1)}, bf16[1,2,256,2048]{3,2,1,0:T(8,128)(2,1)S(1)}, u32[]{:S(2)}, u32[]{:S(2)}) collective-permute-start(bf16[1,2,256,2048]{3,2,1,0:T(8,128)(2,1)} %get-tuple-element.125.refs_9_), channel_id=1, source_target_pairs={{0,8},{4,20},{8,0},{12,28},{16,24},{20,4},{24,16},{28,12},{1,9},{5... | collective-permute-start | bytes 6291464 | tf_op jit(solution)/shard_map/ppermute | solution.py:730
  269.9 18.3 %collective-permute-start.26 = (bf16[2,8,80,128]{3,2,1,0:T(8,128)(2,1)S(1)}, bf16[2,8,80,128]{3,2,1,0:T(8,128)(2,1)S(1)}, u32[]{:S(2)}, u32[]{:S(2)}) collective-permute-start(bf16[2,8,80,128]{3,2,1,0:T(8,128)(2,1)S(1)} %convert_element_type.86), channel_id=1, source_target_pairs={{0,4},{4,0},{8,12},{12,8},{16,20},{20,16},{24,28},{28,24},{1,5},{5... | collective-permute-start | bytes 983048 | tf_op jit(solution)/shard_map/ppermute | solution.py:720
  286.7 18.9 %collective-permute-start.28 = (bf16[1,1,256,2048]{3,2,1,0:T(8,128)(2,1)}, bf16[1,1,256,2048]{3,2,1,0:T(8,128)(2,1)S(1)}, u32[]{:S(2)}, u32[]{:S(2)}) collective-permute-start(bf16[1,1,256,2048]{3,2,1,0:T(8,128)(2,1)} %get-tuple-element.133.refs_6_), channel_id=1, source_target_pairs={{0,16},{4,12},{8,24},{12,4},{16,0},{20,28},{24,8},{28,20},{1,17},{... | collective-permute-start | bytes 3145736 | tf_op jit(solution)/shard_map/ppermute | solution.py:730
  289.2 13.6 %collective-permute-start.29 = (bf16[2,8,80,128]{3,2,1,0:T(8,128)(2,1)S(1)}, bf16[2,8,80,128]{3,2,1,0:T(8,128)(2,1)S(1)}, u32[]{:S(2)}, u32[]{:S(2)}) collective-permute-start(bf16[2,8,80,128]{3,2,1,0:T(8,128)(2,1)S(1)} %get-tuple-element.219), channel_id=1, source_target_pairs={{0,8},{4,12},{8,0},{12,4},{16,24},{20,28},{24,16},{28,20},{1,9},{5... | collective-permute-start | bytes 983048 | tf_op jit(solution)/shard_map/ppermute | solution.py:720
  301.3 39.9 %collective-permute-start.31 = (bf16[1,2,256,2048]{3,2,1,0:T(8,128)(2,1)}, bf16[1,2,256,2048]{3,2,1,0:T(8,128)(2,1)S(1)}, u32[]{:S(2)}, u32[]{:S(2)}) collective-permute-start(bf16[1,2,256,2048]{3,2,1,0:T(8,128)(2,1)} %get-tuple-element.134.refs_6_), channel_id=1, source_target_pairs={{0,8},{4,20},{8,0},{12,28},{16,24},{20,4},{24,16},{28,12},{1,9},{5... | collective-permute-start | bytes 6291464 | tf_op jit(solution)/shard_map/ppermute | solution.py:730
  321.6 13.1 %collective-permute-start.30 = (bf16[768,512]{1,0:T(8,128)(2,1)}, bf16[768,512]{1,0:T(8,128)(2,1)S(1)}, u32[]{:S(2)}, u32[]{:S(2)}) collective-permute-start(bf16[768,512]{1,0:T(8,128)(2,1)} %gate.36), channel_id=1, source_target_pairs={{0,4},{4,0},{8,12},{12,8},{16,20},{20,16},{24,28},{28,24},{1,5},{5... | collective-permute-start | bytes 2359304 | tf_op jit(solution)/shard_map/ppermute | solution.py:720
  327.9 18.9 %collective-permute-start.32 = (bf16[2,8,80,128]{3,2,1,0:T(8,128)(2,1)S(1)}, bf16[2,8,80,128]{3,2,1,0:T(8,128)(2,1)S(1)}, u32[]{:S(2)}, u32[]{:S(2)}) collective-permute-start(bf16[2,8,80,128]{3,2,1,0:T(8,128)(2,1)S(1)} %get-tuple-element.213), channel_id=1, source_target_pairs={{0,16},{4,20},{8,24},{12,28},{16,0},{20,4},{24,8},{28,12},{1,17},{... | collective-permute-start | bytes 983048 | tf_op jit(solution)/shard_map/ppermute | solution.py:720
  330.0 33.3 %collective-permute-start.35 = (bf16[2,32,2048]{2,1,0:T(8,128)(2,1)}, bf16[2,32,2048]{2,1,0:T(8,128)(2,1)S(1)}, u32[]{:S(2)}, u32[]{:S(2)}) collective-permute-start(bf16[2,32,2048]{2,1,0:T(8,128)(2,1)} %get-tuple-element.137.refs_7_.refs_4_), channel_id=1, source_target_pairs={{0,1},{1,0},{2,3},{3,2},{4,5},{5,4},{6,7},{7,6},{8,9},{9,8},{10,11... | collective-permute-start | bytes 786440 | tf_op jit(solution)/shard_map/ppermute | solution.py:720
  331.4 31.9 %collective-permute-start.36 = (bf16[2,32,2048]{2,1,0:T(8,128)(2,1)}, bf16[2,32,2048]{2,1,0:T(8,128)(2,1)S(1)}, u32[]{:S(2)}, u32[]{:S(2)}) collective-permute-start(bf16[2,32,2048]{2,1,0:T(8,128)(2,1)} %get-tuple-element.138.refs_8_.refs_5_), channel_id=1, source_target_pairs={{0,2},{1,3},{2,0},{3,1},{4,6},{5,7},{6,4},{7,5},{8,10},{9,11},{10,... | collective-permute-start | bytes 786440 | tf_op jit(solution)/shard_map/ppermute | solution.py:720
  334.8 28.6 %collective-permute-start.37 = (bf16[2,32,2048]{2,1,0:T(8,128)(2,1)}, bf16[2,32,2048]{2,1,0:T(8,128)(2,1)S(1)}, u32[]{:S(2)}, u32[]{:S(2)}) collective-permute-start(bf16[2,32,2048]{2,1,0:T(8,128)(2,1)} %get-tuple-element.139.refs_9_.refs_6_), channel_id=1, source_target_pairs={{0,3},{1,2},{2,1},{3,0},{4,7},{5,6},{6,5},{7,4},{8,11},{9,10},{10,... | collective-permute-start | bytes 786440 | tf_op jit(solution)/shard_map/ppermute | solution.py:720
  341.2 18.4 %collective-permute-start.33 = (bf16[1,2,256,512]{3,2,1,0:T(8,128)(2,1)}, bf16[1,2,256,512]{3,2,1,0:T(8,128)(2,1)S(1)}, u32[]{:S(2)}, u32[]{:S(2)}) collective-permute-start(bf16[1,2,256,512]{3,2,1,0:T(8,128)(2,1)} %get-tuple-element.145.refs_6_), channel_id=1, source_target_pairs={{0,8},{4,20},{8,0},{12,28},{16,24},{20,4},{24,16},{28,12},{1,9},{5... | collective-permute-start | bytes 1572872 | tf_op jit(solution)/shard_map/ppermute | solution.py:730
  346.8 19.0 %collective-permute-start.34 = (bf16[1,1,256,2048]{3,2,1,0:T(8,128)(2,1)}, bf16[1,1,256,2048]{3,2,1,0:T(8,128)(2,1)S(1)}, u32[]{:S(2)}, u32[]{:S(2)}) collective-permute-start(bf16[1,1,256,2048]{3,2,1,0:T(8,128)(2,1)} %get-tuple-element.146.refs_7_), channel_id=1, source_target_pairs={{0,16},{4,12},{8,24},{12,4},{16,0},{20,28},{24,8},{28,20},{1,17},{... | collective-permute-start | bytes 3145736 | tf_op jit(solution)/shard_map/ppermute | solution.py:730
  374.8 28.8 %collective-permute-start.39 = (bf16[3,768,512]{2,1,0:T(8,128)(2,1)}, bf16[3,768,512]{2,1,0:T(8,128)(2,1)S(1)}, u32[]{:S(2)}, u32[]{:S(2)}) collective-permute-start(bf16[3,768,512]{2,1,0:T(8,128)(2,1)} %get-tuple-element.156.refs_1_), channel_id=1, source_target_pairs={{0,4},{4,0},{8,12},{12,8},{16,20},{20,16},{24,28},{28,24},{1,5},{5... | collective-permute-start | bytes 7077896 | tf_op jit(solution)/shard_map/ppermute | solution.py:720
  374.9 6.4 %collective-permute-start.38 = (bf16[1,1,256,512]{3,2,1,0:T(8,128)(2,1)S(1)}, bf16[1,1,256,512]{3,2,1,0:T(8,128)(2,1)S(1)}, u32[]{:S(2)}, u32[]{:S(2)}) collective-permute-start(bf16[1,1,256,512]{3,2,1,0:T(8,128)(2,1)S(1)} %copy-done.57), channel_id=1, source_target_pairs={{0,16},{4,12},{8,24},{12,4},{16,0},{20,28},{24,8},{28,20},{1,17},{... | collective-permute-start | bytes 786440 | tf_op jit(solution)/shard_map/ppermute | solution.py:730
  385.5 16.1 %collective-permute-start.40 = (bf16[2,32,2560]{2,1,0:T(8,128)(2,1)}, bf16[2,32,2560]{2,1,0:T(8,128)(2,1)S(1)}, u32[]{:S(2)}, u32[]{:S(2)}) collective-permute-start(bf16[2,32,2560]{2,1,0:T(8,128)(2,1)} %get-tuple-element.163.refs_8_), channel_id=1, source_target_pairs={{0,1},{1,0},{2,3},{3,2},{4,5},{5,4},{6,7},{7,6},{8,9},{9,8},{10,11... | collective-permute-start | bytes 983048 | tf_op jit(solution)/shard_map/ppermute | solution.py:720
  385.5 17.4 %collective-permute-start.41 = (bf16[2,32,2560]{2,1,0:T(8,128)(2,1)}, bf16[2,32,2560]{2,1,0:T(8,128)(2,1)S(1)}, u32[]{:S(2)}, u32[]{:S(2)}) collective-permute-start(bf16[2,32,2560]{2,1,0:T(8,128)(2,1)} %get-tuple-element.164.refs_9_), channel_id=1, source_target_pairs={{0,2},{1,3},{2,0},{3,1},{4,6},{5,7},{6,4},{7,5},{8,10},{9,11},{10,... | collective-permute-start | bytes 983048 | tf_op jit(solution)/shard_map/ppermute | solution.py:720
  414.5 21.6 %collective-permute-start.45 = (bf16[3,2,256,512]{3,2,1,0:T(8,128)(2,1)}, bf16[3,2,256,512]{3,2,1,0:T(8,128)(2,1)S(1)}, u32[]{:S(2)}, u32[]{:S(2)}) collective-permute-start(bf16[3,2,256,512]{3,2,1,0:T(8,128)(2,1)} %get-tuple-element.171.refs_8_), channel_id=1, source_target_pairs={{0,8},{4,20},{8,0},{12,28},{16,24},{20,4},{24,16},{28,12},{1,9},{5... | collective-permute-start | bytes 4718600 | tf_op jit(solution)/shard_map/ppermute | solution.py:730
  415.9 12.2 %collective-permute-start.42 = (bf16[2,32,2560]{2,1,0:T(8,128)(2,1)S(1)}, bf16[2,32,2560]{2,1,0:T(8,128)(2,1)S(1)}, u32[]{:S(2)}, u32[]{:S(2)}) collective-permute-start(bf16[2,32,2560]{2,1,0:T(8,128)(2,1)S(1)} %copy-done.56), channel_id=1, source_target_pairs={{0,3},{1,2},{2,1},{3,0},{4,7},{5,6},{6,5},{7,4},{8,11},{9,10},{10,... | collective-permute-start | bytes 983048 | tf_op jit(solution)/shard_map/ppermute | solution.py:720
  428.1 1.5 collective-permute-start.43
  430.3 5.1 %collective-permute-start.44 = (f32[4,1024]{1,0:T(4,128)S(1)}, f32[4,1024]{1,0:T(4,128)S(1)}, u32[]{:S(2)}, u32[]{:S(2)}) collective-permute-start(f32[4,1024]{1,0:T(4,128)S(1)} %fusion.17), channel_id=1, source_target_pairs={{0,8},{4,12},{8,0},{12,4},{16,24},{20,28},{24,16},{28,20},{1,9},{5... | collective-permute-start | bytes 49160 | tf_op jit(solution)/shard_map/ppermute | solution.py:720
  441.4 19.6 %collective-permute-start.49 = (bf16[3,1,256,512]{3,2,1,0:T(8,128)(2,1)}, bf16[3,1,256,512]{3,2,1,0:T(8,128)(2,1)S(1)}, u32[]{:S(2)}, u32[]{:S(2)}) collective-permute-start(bf16[3,1,256,512]{3,2,1,0:T(8,128)(2,1)} %get-tuple-element.177.refs_1_), channel_id=1, source_target_pairs={{0,16},{4,12},{8,24},{12,4},{16,0},{20,28},{24,8},{28,20},{1,17},{... | collective-permute-start | bytes 2359304 | tf_op jit(solution)/shard_map/ppermute | solution.py:730
  443.4 13.9 %collective-permute-start.62 = (f32[1,32,2048]{2,1,0:T(8,128)S(1)}, f32[1,32,2048]{2,1,0:T(8,128)S(1)}, u32[]{:S(2)}, u32[]{:S(2)}) collective-permute-start(f32[1,32,2048]{2,1,0:T(8,128)S(1)} %constant_dynamic-slice_fusion.5), channel_id=1, source_target_pairs={{0,4},{4,0},{8,12},{12,8},{16,20},{20,16},{24,28},{28,24},{1,5},{5... | collective-permute-start | bytes 786440 | tf_op jit(solution)/shard_map/ppermute | solution.py:720
  443.5 10.5 %collective-permute-start.46 = (f32[4,1024]{1,0:T(4,128)}, f32[4,1024]{1,0:T(4,128)S(1)}, u32[]{:S(2)}, u32[]{:S(2)}) collective-permute-start(f32[4,1024]{1,0:T(4,128)} %gate.41), channel_id=1, source_target_pairs={{0,16},{4,20},{8,24},{12,28},{16,0},{20,4},{24,8},{28,12},{1,17},{... | collective-permute-start | bytes 49160 | tf_op jit(solution)/shard_map/ppermute | solution.py:720
  454.7 4.5 collective-permute-start.47
  459.2 11.9 %collective-permute-start.48 = (f32[4,1024]{1,0:T(4,128)S(1)}, f32[4,1024]{1,0:T(4,128)S(1)}, u32[]{:S(2)}, u32[]{:S(2)}) collective-permute-start(f32[4,1024]{1,0:T(4,128)S(1)} %add.279), channel_id=1, source_target_pairs={{0,2},{1,3},{2,0},{3,1},{4,6},{5,7},{6,4},{7,5},{8,10},{9,11},{10,... | collective-permute-start | bytes 49160 | tf_op jit(solution)/shard_map/ppermute | solution.py:720
  464.6 7.8 %collective-permute-start.50 = (bf16[6,32,512]{2,1,0:T(8,128)(2,1)}, bf16[6,32,512]{2,1,0:T(8,128)(2,1)S(1)}, u32[]{:S(2)}, u32[]{:S(2)}) collective-permute-start(bf16[6,32,512]{2,1,0:T(8,128)(2,1)} %get-tuple-element.180), channel_id=1, source_target_pairs={{0,1},{1,0},{2,3},{3,2},{4,5},{5,4},{6,7},{7,6},{8,9},{9,8},{10,11... | collective-permute-start | bytes 589832 | tf_op jit(solution)/shard_map/ppermute | solution.py:720
  465.1 11.0 %collective-permute-start.51 = (bf16[6,32,512]{2,1,0:T(8,128)(2,1)}, bf16[6,32,512]{2,1,0:T(8,128)(2,1)S(1)}, u32[]{:S(2)}, u32[]{:S(2)}) collective-permute-start(bf16[6,32,512]{2,1,0:T(8,128)(2,1)} %get-tuple-element.181), channel_id=1, source_target_pairs={{0,2},{1,3},{2,0},{3,1},{4,6},{5,7},{6,4},{7,5},{8,10},{9,11},{10,... | collective-permute-start | bytes 589832 | tf_op jit(solution)/shard_map/ppermute | solution.py:720
  467.7 8.4 %collective-permute-start.52 = (bf16[6,32,512]{2,1,0:T(8,128)(2,1)}, bf16[6,32,512]{2,1,0:T(8,128)(2,1)S(1)}, u32[]{:S(2)}, u32[]{:S(2)}) collective-permute-start(bf16[6,32,512]{2,1,0:T(8,128)(2,1)} %get-tuple-element.182), channel_id=1, source_target_pairs={{0,3},{1,2},{2,1},{3,0},{4,7},{5,6},{6,5},{7,4},{8,11},{9,10},{10,... | collective-permute-start | bytes 589832 | tf_op jit(solution)/shard_map/ppermute | solution.py:720
  469.8 21.9 %collective-permute-start.61 = (f32[1,32,2560]{2,1,0:T(8,128)}, f32[1,32,2560]{2,1,0:T(8,128)}, u32[]{:S(2)}, u32[]{:S(2)}) collective-permute-start(f32[1,32,2560]{2,1,0:T(8,128)} %constant_dynamic-slice_fusion.2), channel_id=1, source_target_pairs={{0,4},{4,0},{8,12},{12,8},{16,20},{20,16},{24,28},{28,24},{1,5},{5... | collective-permute-start | bytes 983048 | tf_op jit(solution)/shard_map/ppermute | solution.py:720
  479.3 6.5 %collective-permute-start.53 = (f32[8,128]{1,0:T(8,128)S(1)}, f32[8,128]{1,0:T(8,128)S(1)}, u32[]{:S(2)}, u32[]{:S(2)}) collective-permute-start(f32[8,128]{1,0:T(8,128)S(1)} %broadcast_in_dim.37), channel_id=1, source_target_pairs={{0,1},{1,0},{2,3},{3,2},{4,5},{5,4},{6,7},{7,6},{8,9},{9,8},{10,11... | collective-permute-start | bytes 12296 | tf_op jit(solution)/shard_map/ppermute | solution.py:720
  482.1 4.5 collective-permute-start.54
  482.8 5.4 %collective-permute-start.55 = (f32[8,128]{1,0:T(8,128)S(1)}, f32[8,128]{1,0:T(8,128)S(1)}, u32[]{:S(2)}, u32[]{:S(2)}) collective-permute-start(f32[8,128]{1,0:T(8,128)S(1)} %broadcast_in_dim.37), channel_id=1, source_target_pairs={{0,3},{1,2},{2,1},{3,0},{4,7},{5,6},{6,5},{7,4},{8,11},{9,10},{10,... | collective-permute-start | bytes 12296 | tf_op jit(solution)/shard_map/ppermute | solution.py:720
  488.2 4.6 collective-permute-start.56
  489.0 3.9 collective-permute-start.57
  490.0 4.5 collective-permute-start.58
  495.2 6.9 %collective-permute-start.60 = (f32[3,32,512]{2,1,0:T(8,128)}, f32[3,32,512]{2,1,0:T(8,128)}, u32[]{:S(2)}, u32[]{:S(2)}) collective-permute-start(f32[3,32,512]{2,1,0:T(8,128)} %dynamic-slice_bitcast_fusion), channel_id=1, source_target_pairs={{0,4},{4,0},{8,12},{12,8},{16,20},{20,16},{24,28},{28,24},{1,5},{5... | collective-permute-start | bytes 589832 | tf_op jit(solution)/shard_map/ppermute | solution.py:720
  (74 other events, 424.4 us)
Sparse Core Ops, SparseCore 0:
  62.1 28.7 all-gather.2
  120.6 28.8 all-gather.4
where the time goes:
time: 521 us; the launch traced here: 513 us
  Pallas kernels  229 us (44%)
  waiting for transfers between devices  119 us (23%)
  starting transfers between devices  68.4 us (13%)
  other arithmetic  39.1 us (8%)
  local copies, waits for them, and re-layouts  37.7 us (7%)
  between operations  19.8 us (4%)
    pallas_call x16, Pallas kernels, launch_at(): call(spot.reshape(-1).astype(jnp.int32), *args, *tokens)  155 us
    pallas_call x36, Pallas kernels, launch(): return lambda *args: call(*args, *tokens)  74.6 us
    ppermute x49, waiting for transfers between devices, flip(): lax.ppermute(array, axis, [(i, i ^ bit) for i in range(lax.axis_size(axis...  64.6 us
    ppermute x14, waiting for transfers between devices, flip_pos(): return lax.ppermute(array, 'seq', pairs)  54.2 us
    ppermute x49, starting transfers between devices, flip(): lax.ppermute(array, axis, [(i, i ^ bit) for i in range(lax.axis_size(axis...  52 us
    unnamed x146, local copies, waits for them, and re-layouts  29.2 us
    ppermute x14, starting transfers between devices, flip_pos(): return lax.ppermute(array, 'seq', pairs)  16.3 us
  transfers between devices with their start and end apart: 65, of which 25 were waited for; matrix products, arithmetic and copies ran while one was open for 8% of the time, Pallas kernels for 39%

commit v1 on v0

--- a/solution.py
+++ b/solution.py
@@ -1176,23 +1176,19 @@
         late[0], late[1], resid, e, vec, wo, mixed, rden, fq, count, span, marks + [late_other]
     )
     later = Passing(dstate, True, False)
-    marks = [dstate, later.outside]
+    branch_other = flip_core(branch_send)
+    marks = weigh(outs[0], mixed_t, mixed_t_other, branch[None], branch_other[None], [dstate, later.outside])
     for _ in range(stages - 1):
-        marks = marks + advance(firsts, [dstate])
+        marks = marks + advance(firsts, [outs[0].kept])
     marks = weigh(seconds[0], lt, lt_other, late[2][None], late_other[None], marks)
-    passed = later.hop([seconds[0].kept])
     firsts_last = Last(firsts, [seconds[0].kept])
-    parts = [attend_back(0, fq, fk, v, dn, w, prior, span, marks + firsts_last.sends + [passed])]
-    branch_other = flip_core(gate([branch_send], [parts[0][0]])[0])
-    settled = firsts_last.sends
-    marks = weigh(outs[0], mixed_t, mixed_t_other, branch[None], branch_other[None], settled)
+    parts = [attend_back(0, fq, fk, v, dn, w, prior, span, marks + firsts_last.sends)]
+    marks = [later.hop([parts[0][0]])]
     for _ in range(stages - 1):
-        marks = marks + advance(seconds, [parts[0][0]])
+        marks = marks + advance(seconds + outs, [parts[0][0]])
     for image in range(1, count):
         parts.append(attend_back(image, fq, fk, v, dn, w, prior, span, marks))
-    for _ in range(stages - 1):
-        marks = advance(outs, [parts[-1][0]])
-    marks = marks + seconds[0].came + firsts_last.settle(slice(0, None), [parts[-1][0]])
+    marks = seconds[0].came + outs[0].came + firsts_last.settle(slice(0, None), [parts[-1][0]])
     while later.bits:
         later.hop([parts[-1][0]])
     later = later.outside

time: 521 us -> 518 us (level)
    ppermute x14, waiting for transfers between devices: 54.2 us -> 42.9 us  [flip_pos(): return lax.ppermute(array, 'seq', pairs)]
    ppermute x49, waiting for transfers between devices: 64.6 us -> 74.7 us  [flip(): lax.ppermute(array, axis, [(i, i ^ bit) for i in range(lax.axis_size(axis...]
    unnamed x146 -> x144, local copies, waits for them, and re-layouts: 29.2 us -> 25.6 us
    pallas_call x16 -> x15, Pallas kernels: 155 us -> 152 us  [launch_at(): call(spot.reshape(-1).astype(jnp.int32), *args, *tokens)]
    pallas_call x36 -> x35, Pallas kernels: 74.6 us -> 74.9 us  [launch(): return lambda *args: call(*args, *tokens)]
  transfers between devices with their start and end apart: 65 -> 65, of which waited for: 25 -> 26; matrix products, arithmetic and copies ran while one was open for 8% -> 9% of each run, Pallas kernels for 39% -> 38%
where the time goes in v1:
time: 518 us; the launch traced here: 509 us
  Pallas kernels  227 us (44%)
  waiting for transfers between devices  118 us (23%)
  starting transfers between devices  67.8 us (13%)
  other arithmetic  43.1 us (8%)
  local copies, waits for them, and re-layouts  34.1 us (7%)
  between operations  19.8 us (4%)
    pallas_call x15, Pallas kernels, launch_at(): call(spot.reshape(-1).astype(jnp.int32), *args, *tokens)  152 us
    pallas_call x35, Pallas kernels, launch(): return lambda *args: call(*args, *tokens)  74.9 us
    ppermute x49, waiting for transfers between devices, flip(): lax.ppermute(array, axis, [(i, i ^ bit) for i in range(lax.axis_size(axis...  74.7 us
    ppermute x49, starting transfers between devices, flip(): lax.ppermute(array, axis, [(i, i ^ bit) for i in range(lax.axis_size(axis...  50.5 us
    ppermute x14, waiting for transfers between devices, flip_pos(): return lax.ppermute(array, 'seq', pairs)  42.9 us
    unnamed x144, local copies, waits for them, and re-layouts  25.6 us
    ppermute x14, starting transfers between devices, flip_pos(): return lax.ppermute(array, 'seq', pairs)  17.2 us
  transfers between devices with their start and end apart: 65, of which 26 were waited for; matrix products, arithmetic and copies ran while one was open for 9% of the time, Pallas kernels for 38%

profile of v1, /device:TPU:0, one launch (start us, length us, event | category | flops | bytes accessed | tf_op | source)
XLA Modules:
  0.0 509.3 jit_solution(10674179007355336646)
XLA Ops:
  10.8 4.0 collective-permute-start.2
  16.4 12.2 %collective-permute-done.2.refs_1_ = bf16[2,2,32,1152]{3,2,1,0:T(8,128)(2,1)S(1)} collective-permute-done((bf16[2,2,32,1152]{3,2,1,0:T(8,128)(2,1)S(1)}, bf16[2,2,32,1152]{3,2,1,0:T(8,128)(2,1)S(1)}, u32[]{:S(2)}, u32[]{:S(2)}) %collective-permute-start.2) | collective-permute-done | bytes 294944 | tf_op jit(solution)/shard_map/ppermute | solution.py:720
  29.2 2.5 turn.1.refs_3_
  31.7 5.3 %collective-permute-done.3.refs_2_ = bf16[2,2,32,1152]{3,2,1,0:T(8,128)(2,1)S(1)} collective-permute-done((bf16[2,2,32,1152]{3,2,1,0:T(8,128)(2,1)S(1)}, bf16[2,2,32,1152]{3,2,1,0:T(8,128)(2,1)S(1)}, u32[]{:S(2)}, u32[]{:S(2)}) %collective-permute-start.3) | collective-permute-done | bytes 294944 | tf_op jit(solution)/shard_map/ppermute | solution.py:720
  37.8 2.3 assemble.6
  41.3 2.0 narrow.1
  43.4 13.1 %collective-permute-done.4.refs_0_ = bf16[2,1,256,1152]{3,2,1,0:T(8,128)(2,1)S(1)} collective-permute-done((bf16[2,1,256,1152]{3,2,1,0:T(8,128)(2,1)}, bf16[2,1,256,1152]{3,2,1,0:T(8,128)(2,1)S(1)}, u32[]{:S(2)}, u32[]{:S(2)}) %collective-permute-start.4) | collective-permute-done | bytes 1179680 | tf_op jit(solution)/shard_map/ppermute | solution.py:730
  57.6 3.1 assemble.7
  62.1 27.6 %collective-permute-done.6.refs_0_ = bf16[2,2,256,1152]{3,2,1,0:T(8,128)(2,1)S(1)} collective-permute-done((bf16[2,2,256,1152]{3,2,1,0:T(8,128)(2,1)}, bf16[2,2,256,1152]{3,2,1,0:T(8,128)(2,1)S(1)}, u32[]{:S(2)}, u32[]{:S(2)}) %collective-permute-start.6) | collective-permute-done | bytes 2359328 | tf_op jit(solution)/shard_map/ppermute | solution.py:730
  91.2 2.1 fusion.26
  93.8 2.7 collective-permute-done.8.refs_2_
  97.3 2.2 assemble.8
  104.4 11.3 %project.1 = (bf16[768,1024]{1,0:T(8,128)(2,1)}, bf16[768,1024]{1,0:T(8,128)(2,1)}, bf16[768,1024]{1,0:T(8,128)(2,1)}, bf16[1024,768]{1,0:T(8,128)(2,1)}, f32[2,...) custom-call(s32[3]{0:T(128)} %pad_add_fusion.spot_ref, bf16[768,1024]{1,0:T(8,128)(2,1)} %bitcast.92, ...), custom_call_target="tpu_custom_call" | custom-call | flops 3221225472 | bytes 17825792 | tf_op jit(solution)/shard_map/project/pallas_call | solution.py:73
  116.7 3.0 assemble.9
  120.5 4.4 collective-permute-done.9
  128.0 7.7 %query.1 = (bf16[768,1024]{1,0:T(8,128)(2,1)}, bf16[1024,1024]{1,0:T(8,128)(2,1)}, bf16[1024,1024]{1,0:T(8,128)(2,1)}) custom-call(s32[3]{0:T(128)} %pad_add_fusion.spot_ref, bf16[768,1024]{1,0:T(8,128)(2,1)} %get-tuple-element.103.refs_0_, bf16[2,512,1152]{2,1,0:T(8,128)(2,1)} %bitcast.87, bf16[2,512,1152]{2,1,0:T(8,128)(2,1)} %bitcast.90, ...), custom_call_target="tpu_custom_call" | custom-call | flops 1610612736 | bytes 9437184 | tf_op jit(solution)/shard_map/query/pallas_call | solution.py:73
  137.4 2.1 fusion.2
  139.5 11.1 %attend.1 = (f32[768,1024]{1,0:T(8,128)}, f32[768,1024]{1,0:T(8,128)}) custom-call(bf16[768,1024]{1,0:T(8,128)(2,1)} %get-tuple-element.106.refs_1_.refs_0_.refs_3_.refs_8_, bf16[768,1024]{1,0:T(8,128)(2,1)} %get-tuple-element.107.refs_1_.refs_6_, bf16[768,1024]{1,0:T(8,128)(2,1)} %get-tuple-element.108.refs_2_.refs_7_, ...), custom_call_target="tpu_custom_call" | custom-call | flops 9663676416 | bytes 11010048 | tf_op jit(solution)/shard_map/attend/pallas_call | solution.py:52
  150.6 2.1 fusion.25
  155.4 2.2 assemble.10
  158.7 4.5 collective-permute-done.14.refs_0_
  165.8 10.0 %mix.1 = (bf16[768,1024]{1,0:T(8,128)(2,1)}, f32[768,1024]{1,0:T(8,128)}, f32[768,1024]{1,0:T(8,128)}, bf16[768,1024]{1,0:T(8,128)(2,1)}, bf16[1024,768]{1,0:T(8,128)(2,1)}, /*index=5*/bf16[1024,768]{1,0:T(8,128)(2,1)}) custom-call(bf16[768,1024]{1,0:T(8,128)(2,1)} %bitcast.93, f32[4,1024]{1,0:T(4,128)} %bitcast.136, ...), custom_call_target="tpu_custom_call" | custom-call | flops 6442450944 | bytes 20971520 | tf_op jit(solution)/shard_map/mix/pallas_call | solution.py:52
  175.9 2.9 assemble.11
  180.9 2.5 collective-permute-done.20.refs_7_.refs_0_
  184.7 21.5 %feed.2 = (f32[768,1024]{1,0:T(8,128)}, f32[768,1024]{1,0:T(8,128)}, bf16[768,2048]{1,0:T(8,128)(2,1)}, bf16[768,2048]{1,0:T(8,128)(2,1)}) custom-call(s32[3]{0:T(128)} %pad_add_fusion.spot_ref, bf16[768,1024]{1,0:T(8,128)(2,1)} %get-tuple-element.113.refs_0_, bf16[768,1024]{1,0:T(8,128)(2,1)} %bitcast.119, bf16[2,512,1024]{2,1,0:T(8,128)(2,1)} %bitcast.104, ...), custom_call_target="tpu_custom_call" | custom-call | flops 12884901888 | bytes 30408704 | tf_op jit(solution)/shard_map/feed/pallas_call | solution.py:73
  211.9 2.3 collective-permute-done.22.refs_8_.refs_1_
  214.2 4.5 collective-permute-done.23.refs_9_.refs_1_
  219.9 22.8 %feed.3 = (f32[768,1024]{1,0:T(8,128)}, f32[768,1024]{1,0:T(8,128)}, bf16[768,2048]{1,0:T(8,128)(2,1)}, bf16[768,2048]{1,0:T(8,128)(2,1)}) custom-call(s32[3]{0:T(128)} %pad_add_fusion.spot_ref, bf16[768,1024]{1,0:T(8,128)(2,1)} %get-tuple-element.113.refs_0_, bf16[768,1024]{1,0:T(8,128)(2,1)} %bitcast.120, bf16[2,512,1024]{2,1,0:T(8,128)(2,1)} %bitcast.116, ...), custom_call_target="tpu_custom_call" | custom-call | flops 12884901888 | bytes 30408704 | tf_op jit(solution)/shard_map/feed/pallas_call | solution.py:73
  243.8 11.4 %weigh.4 = (bf16[1,2,256,2048]{3,2,1,0:T(8,128)(2,1)}, bf16[1,2,256,2048]{3,2,1,0:T(8,128)(2,1)}) custom-call(s32[4]{0:T(128)} %pad_add_fusion.1.spot_ref, bf16[1024,768]{1,0:T(8,128)(2,1)} %get-tuple-element.203.refs_0_, bf16[1024,768]{1,0:T(8,128)(2,1)} %copy-done.69, bf16[1,768,2048]{2,1,0:T(8,128)(2,1)} %bitcast.144, ...), custom_call_target="tpu_custom_call" | custom-call | flops 6442450944 | bytes 17825792 | tf_op jit(solution)/shard_map/weigh/pallas_call | solution.py:73
  256.2 13.2 %turn_back.1 = (bf16[768,1024]{1,0:T(8,128)(2,1)}, f32[768,1024]{1,0:T(8,128)}, bf16[768,512]{1,0:T(8,128)(2,1)}, bf16[768,512]{1,0:T(8,128)(2,1)}, bf16[768,102...) custom-call(s32[1]{0:T(128)} %bitcast.refs_0_.spot_ref, ...), custom_call_target="tpu_custom_call" | custom-call | flops 8053063680 | bytes 23592960 | tf_op jit(solution)/shard_map/turn_back/pallas_call | solution.py:73
  273.5 2.1 fusion.7
  276.5 5.6 %weigh.5 = (bf16[1,2,256,512]{3,2,1,0:T(8,128)(2,1)}, bf16[1,2,256,512]{3,2,1,0:T(8,128)(2,1)}) custom-call(s32[4]{0:T(128)} %pad_add_fusion.1.spot_ref, bf16[1024,768]{1,0:T(8,128)(2,1)} %get-tuple-element.118.refs_0_, bf16[1024,768]{1,0:T(8,128)(2,1)} %copy-done.28, bf16[1,768,512]{2,1,0:T(8,128)(2,1)} %bitcast.127, bf16[1,768,512]{2,1,0:T(8,128)(2,1)} %bitcast.128, ...), custom_call_target="tpu_custom_call" | custom-call | flops 1610612736 | bytes 6815744 | tf_op jit(solution)/shard_map/weigh/pallas_call | solution.py:73
  283.4 4.1 fold.3
  288.6 11.4 %weigh.6 = (bf16[1,2,256,2048]{3,2,1,0:T(8,128)(2,1)}, bf16[1,2,256,2048]{3,2,1,0:T(8,128)(2,1)}) custom-call(s32[4]{0:T(128)} %pad_add_fusion.1.spot_ref, bf16[1024,768]{1,0:T(8,128)(2,1)} %get-tuple-element.203.refs_0_, bf16[1024,768]{1,0:T(8,128)(2,1)} %copy-done.69, bf16[1,768,2048]{2,1,0:T(8,128)(2,1)} %bitcast.143, ...), custom_call_target="tpu_custom_call" | custom-call | flops 6442450944 | bytes 17825792 | tf_op jit(solution)/shard_map/weigh/pallas_call | solution.py:73
  306.4 3.1 last.3
  310.8 3.3 collective-permute-start.37
  314.2 12.2 %attend_back.2 = (bf16[384,1024]{1,0:T(8,128)(2,1)}, f32[384,1024]{1,0:T(8,128)}, f32[384,1024]{1,0:T(8,128)}) custom-call(bf16[768,1024]{1,0:T(8,128)(2,1)} %get-tuple-element.106.refs_1_.refs_0_.refs_3_.refs_8_, bf16[768,1024]{1,0:T(8,128)(2,1)} %get-tuple-element.107.refs_1_.refs_6_, bf16[768,1024]{1,0:T(8,128)(2,1)} %get-tuple-element.108.refs_2_.refs_7_, ...), custom_call_target="tpu_custom_call" | custom-call | flops 9663676416 | bytes 9437184 | tf_op jit(solution)/shard_map/attend_back/pallas_call | solution.py:52
  326.4 6.9 %collective-permute-done.30.refs_0_ = bf16[2,8,80,128]{3,2,1,0:T(8,128)(2,1)S(1)} collective-permute-done((bf16[2,8,80,128]{3,2,1,0:T(8,128)(2,1)}, bf16[2,8,80,128]{3,2,1,0:T(8,128)(2,1)S(1)}, u32[]{:S(2)}, u32[]{:S(2)}) %collective-permute-start.30) | collective-permute-done | bytes 327712 | tf_op jit(solution)/shard_map/ppermute | solution.py:720
  333.3 4.2 collective-permute-start.38
  337.5 2.0 fusion.4
  341.8 4.7 fold.4
  347.6 12.1 %attend_back.3 = (bf16[384,1024]{1,0:T(8,128)(2,1)}, f32[384,1024]{1,0:T(8,128)}, f32[384,1024]{1,0:T(8,128)}) custom-call(bf16[768,1024]{1,0:T(8,128)(2,1)} %get-tuple-element.106.refs_1_.refs_0_.refs_3_.refs_8_, bf16[768,1024]{1,0:T(8,128)(2,1)} %get-tuple-element.107.refs_1_.refs_6_, bf16[768,1024]{1,0:T(8,128)(2,1)} %get-tuple-element.108.refs_2_.refs_7_, ...), custom_call_target="tpu_custom_call" | custom-call | flops 9663676416 | bytes 9437184 | tf_op jit(solution)/shard_map/attend_back/pallas_call | solution.py:52
  364.1 2.0 collective-permute-done.35.refs_10_
  367.2 8.0 %finish.1 = (bf16[3,768,512]{2,1,0:T(8,128)(2,1)}, bf16[3,768,512]{2,1,0:T(8,128)(2,1)}) custom-call(s32[1]{0:T(128)} %bitcast.refs_0_.spot_ref, bf16[384,1024]{1,0:T(8,128)(2,1)} %get-tuple-element.144.refs_1_.refs_8_.refs_0_, f32[384,1024]{1,0:T(8,128)} %get-tuple-element.145.refs_1_, f32[384,1024]{1,0:T(8,128)} %get-tuple-element.146.refs_2_, ...), custom_call_target="tpu_custom_call" | custom-call | flops 805306368 | bytes 18874368 | tf_op jit(solution)/shard_map/finish/pallas_call | solution.py:73
  375.3 3.5 last.4
  379.6 3.4 collective-permute-start.41
  384.6 8.4 %enter.2 = (bf16[384,1024]{1,0:T(8,128)(2,1)}, f32[8,1024]{1,0:T(8,128)}) custom-call(s32[1]{0:T(128)} %bitcast.refs_0_.spot_ref, bf16[3,768,512]{2,1,0:T(8,128)(2,1)} %get-tuple-element.155.refs_5_.refs_0_.refs_2_, bf16[3,768,512]{2,1,0:T(8,128)(2,1)} %get-tuple-element.156.refs_1_, bf16[1024,1024]{1,0:T(8,128)(2,1)} %get-tuple-element.157.refs_2_, ...), custom_call_target="tpu_custom_call" | custom-call | flops 2415919104 | bytes 11796480 | tf_op jit(solution)/shard_map/enter/pallas_call | solution.py:73
  393.0 2.9 collective-permute-done.40.refs_0_
  395.9 2.4 collective-permute-done.41.refs_1_
  400.5 9.4 %weigh.7 = (bf16[3,2,256,512]{3,2,1,0:T(8,128)(2,1)}, bf16[3,2,256,512]{3,2,1,0:T(8,128)(2,1)}) custom-call(s32[4]{0:T(128)} %pad_add_fusion.1.spot_ref, bf16[1024,768]{1,0:T(8,128)(2,1)} %get-tuple-element.109.refs_0_, bf16[1024,768]{1,0:T(8,128)(2,1)} %collective-permute-done.13.refs_5_.refs_1_, ...), custom_call_target="tpu_custom_call" | custom-call | flops 4831838208 | bytes 14155776 | tf_op jit(solution)/shard_map/weigh/pallas_call | solution.py:73
  412.2 2.5 collective-permute-start.42
  414.7 8.4 %enter.3 = (bf16[384,1024]{1,0:T(8,128)(2,1)}, f32[8,1024]{1,0:T(8,128)}) custom-call(s32[1]{0:T(128)} %bitcast.refs_0_.spot_ref, bf16[3,768,512]{2,1,0:T(8,128)(2,1)} %get-tuple-element.155.refs_5_.refs_0_.refs_2_, bf16[3,768,512]{2,1,0:T(8,128)(2,1)} %get-tuple-element.156.refs_1_, bf16[1024,1024]{1,0:T(8,128)(2,1)} %get-tuple-element.157.refs_2_, ...), custom_call_target="tpu_custom_call" | custom-call | flops 2415919104 | bytes 11796480 | tf_op jit(solution)/shard_map/enter/pallas_call | solution.py:73
  427.3 2.6 multiply_reduce_fusion
  432.7 4.1 fold.5
  439.1 10.3 %collective-permute-done.46 = f32[4,1024]{1,0:T(4,128)S(1)} collective-permute-done((f32[4,1024]{1,0:T(4,128)}, f32[4,1024]{1,0:T(4,128)S(1)}, u32[]{:S(2)}, u32[]{:S(2)}) %collective-permute-start.46) | collective-permute-done | bytes 16416 | tf_op jit(solution)/shard_map/ppermute | solution.py:720
  450.1 2.6 collective-permute-start.47
  454.5 1.9 collective-permute-start.48
  457.3 2.8 last.5
  460.5 2.7 collective-permute-start.51
  467.9 4.3 collective-permute-done.51
  475.3 2.7 collective-permute-start.53
  478.2 2.2 collective-permute-start.55
  488.4 2.1 collective-permute-done.58
  493.1 4.4 multiply_add_fusion
  (324 shorter events, 105.5 us)
Async XLA Ops:
  7.2 84.0 %all-gather.3.cloned.1.call-start = ((), (), s32[]{:S(2)}) async-start(), calls=%async_computation | async-start | bytes 1310720 | tf_op jit(solution)/shard_map/all_gather | solution.py:1128
  9.2 1.5 collective-permute-start
  10.8 17.8 %collective-permute-start.2 = (bf16[2,2,32,1152]{3,2,1,0:T(8,128)(2,1)S(1)}, bf16[2,2,32,1152]{3,2,1,0:T(8,128)(2,1)S(1)}, u32[]{:S(2)}, u32[]{:S(2)}) collective-permute-start(bf16[2,2,32,1152]{3,2,1,0:T(8,128)(2,1)S(1)} %maximum_select_fusion.refs_1_), channel_id=1, source_target_pairs={{0,2},{1,3},{2,0},{3,1},{4,6},{5,7},{6,4},{7,5},{8,10},{9,11},{10,... | collective-permute-start | bytes 884744 | tf_op jit(solution)/shard_map/ppermute | solution.py:720
  14.8 16.9 %collective-permute-start.1 = (bf16[2,2,32,1152]{3,2,1,0:T(8,128)(2,1)S(1)}, bf16[2,2,32,1152]{3,2,1,0:T(8,128)(2,1)S(1)}, u32[]{:S(2)}, u32[]{:S(2)}) collective-permute-start(bf16[2,2,32,1152]{3,2,1,0:T(8,128)(2,1)S(1)} %maximum_select_fusion.refs_1_), channel_id=1, source_target_pairs={{0,1},{1,0},{2,3},{3,2},{4,5},{5,4},{6,7},{7,6},{8,9},{9,8},{10,11... | collective-permute-start | bytes 884744 | tf_op jit(solution)/shard_map/ppermute | solution.py:720
  28.6 8.5 %collective-permute-start.3 = (bf16[2,2,32,1152]{3,2,1,0:T(8,128)(2,1)S(1)}, bf16[2,2,32,1152]{3,2,1,0:T(8,128)(2,1)S(1)}, u32[]{:S(2)}, u32[]{:S(2)}) collective-permute-start(bf16[2,2,32,1152]{3,2,1,0:T(8,128)(2,1)S(1)} %collective-permute-done.2.refs_1_), channel_id=1, source_target_pairs={{0,1},{1,0},{2,3},{3,2},{4,5},{5,4},{6,7},{7,6},{8,9},{9,8},{10,11... | collective-permute-start | bytes 884744 | tf_op jit(solution)/shard_map/ppermute | solution.py:720
  40.1 16.5 %collective-permute-start.4 = (bf16[2,1,256,1152]{3,2,1,0:T(8,128)(2,1)}, bf16[2,1,256,1152]{3,2,1,0:T(8,128)(2,1)S(1)}, u32[]{:S(2)}, u32[]{:S(2)}) collective-permute-start(bf16[2,1,256,1152]{3,2,1,0:T(8,128)(2,1)} %bitcast.96), channel_id=1, source_target_pairs={{0,8},{4,20},{8,0},{12,28},{16,24},{20,4},{24,16},{28,12},{1,9},{5... | collective-permute-start | bytes 3538952 | tf_op jit(solution)/shard_map/ppermute | solution.py:730
  60.7 29.1 %collective-permute-start.6 = (bf16[2,2,256,1152]{3,2,1,0:T(8,128)(2,1)}, bf16[2,2,256,1152]{3,2,1,0:T(8,128)(2,1)S(1)}, u32[]{:S(2)}, u32[]{:S(2)}) collective-permute-start(bf16[2,2,256,1152]{3,2,1,0:T(8,128)(2,1)} %bitcast.81), channel_id=1, source_target_pairs={{0,16},{4,12},{8,24},{12,4},{16,0},{20,28},{24,8},{28,20},{1,17},{... | collective-permute-start | bytes 7077896 | tf_op jit(solution)/shard_map/ppermute | solution.py:730
  62.0 88.6 %all-gather.5.cloned.1.call-start = ((), (), s32[]{:S(2)}) async-start(), calls=%async_computation.1 | async-start | bytes 1310720 | tf_op jit(solution)/shard_map/all_gather | solution.py:1128
  62.1 39.3 %collective-permute-start.5 = (bf16[2,2,256,1152]{3,2,1,0:T(8,128)(2,1)}, bf16[2,2,256,1152]{3,2,1,0:T(8,128)(2,1)}, u32[]{:S(2)}, u32[]{:S(2)}) collective-permute-start(bf16[2,2,256,1152]{3,2,1,0:T(8,128)(2,1)} %bitcast.82), channel_id=1, source_target_pairs={{0,4},{4,0},{8,12},{12,8},{16,20},{20,16},{24,28},{28,24},{1,5},{5... | collective-permute-start | bytes 7077896 | tf_op jit(solution)/shard_map/ppermute | solution.py:720
  91.2 11.3 %collective-permute-start.7 = (bf16[2,2,256,1152]{3,2,1,0:T(8,128)(2,1)}, bf16[2,2,256,1152]{3,2,1,0:T(8,128)(2,1)S(1)}, u32[]{:S(2)}, u32[]{:S(2)}) collective-permute-start(bf16[2,2,256,1152]{3,2,1,0:T(8,128)(2,1)} %gate.23.refs_1_), channel_id=1, source_target_pairs={{0,4},{4,0},{8,12},{12,8},{16,20},{20,16},{24,28},{28,24},{1,5},{5... | collective-permute-start | bytes 7077896 | tf_op jit(solution)/shard_map/ppermute | solution.py:720
  93.2 3.2 collective-permute-start.8
  99.5 16.3 %collective-permute-start.10 = (bf16[2,1,256,1024]{3,2,1,0:T(8,128)(2,1)}, bf16[2,1,256,1024]{3,2,1,0:T(8,128)(2,1)S(1)}, u32[]{:S(2)}, u32[]{:S(2)}) collective-permute-start(bf16[2,1,256,1024]{3,2,1,0:T(8,128)(2,1)} %gate.24.refs_6_.refs_1_), channel_id=1, source_target_pairs={{0,8},{4,20},{8,0},{12,28},{16,24},{20,4},{24,16},{28,12},{1,9},{5... | collective-permute-start | bytes 3145736 | tf_op jit(solution)/shard_map/ppermute | solution.py:730
  119.7 19.8 %collective-permute-start.12 = (bf16[2,2,256,1024]{3,2,1,0:T(8,128)(2,1)}, bf16[2,2,256,1024]{3,2,1,0:T(8,128)(2,1)}, u32[]{:S(2)}, u32[]{:S(2)}) collective-permute-start(bf16[2,2,256,1024]{3,2,1,0:T(8,128)(2,1)} %bitcast.102), channel_id=1, source_target_pairs={{0,4},{4,0},{8,12},{12,8},{16,20},{20,16},{24,28},{28,24},{1,5},{5... | collective-permute-start | bytes 6291464 | tf_op jit(solution)/shard_map/ppermute | solution.py:720
  119.8 19.7 %collective-permute-start.13 = (bf16[1024,768]{1,0:T(8,128)(2,1)}, bf16[1024,768]{1,0:T(8,128)(2,1)}, u32[]{:S(2)}, u32[]{:S(2)}) collective-permute-start(bf16[1024,768]{1,0:T(8,128)(2,1)} %get-tuple-element.109.refs_0_), channel_id=1, source_target_pairs={{0,4},{4,0},{8,12},{12,8},{16,20},{20,16},{24,28},{28,24},{1,5},{5... | collective-permute-start | bytes 4718600 | tf_op jit(solution)/shard_map/ppermute | solution.py:720
  120.3 4.5 collective-permute-start.9
  125.9 10.8 %collective-permute-start.11 = (bf16[2,8,80,128]{3,2,1,0:T(8,128)(2,1)}, bf16[2,8,80,128]{3,2,1,0:T(8,128)(2,1)S(1)}, u32[]{:S(2)}, u32[]{:S(2)}) collective-permute-start(bf16[2,8,80,128]{3,2,1,0:T(8,128)(2,1)} %get-tuple-element.221), channel_id=1, source_target_pairs={{0,8},{4,12},{8,0},{12,4},{16,24},{20,28},{24,16},{28,20},{1,9},{5... | collective-permute-start | bytes 983048 | tf_op jit(solution)/shard_map/ppermute | solution.py:720
  126.9 48.9 %collective-permute-start.18 = (bf16[2,2,256,1024]{3,2,1,0:T(8,128)(2,1)S(1)}, bf16[2,2,256,1024]{3,2,1,0:T(8,128)(2,1)}, u32[]{:S(2)}, u32[]{:S(2)}) collective-permute-start(bf16[2,2,256,1024]{3,2,1,0:T(8,128)(2,1)S(1)} %bitcast.105), channel_id=1, source_target_pairs={{0,16},{4,12},{8,24},{12,4},{16,0},{20,28},{24,8},{28,20},{1,17},{... | collective-permute-start | bytes 6291464 | tf_op jit(solution)/shard_map/ppermute | solution.py:730
  152.7 1.9 collective-permute-start.15
  152.7 10.5 %collective-permute-start.14 = (bf16[2,8,80,128]{3,2,1,0:T(8,128)(2,1)S(1)}, bf16[2,8,80,128]{3,2,1,0:T(8,128)(2,1)S(1)}, u32[]{:S(2)}, u32[]{:S(2)}) collective-permute-start(bf16[2,8,80,128]{3,2,1,0:T(8,128)(2,1)S(1)} %copy-done.57), channel_id=1, source_target_pairs={{0,16},{4,20},{8,24},{12,28},{16,0},{20,4},{24,8},{28,12},{1,17},{... | collective-permute-start | bytes 983048 | tf_op jit(solution)/shard_map/ppermute | solution.py:720
  157.6 18.2 %collective-permute-start.16 = (bf16[2,1,256,1024]{3,2,1,0:T(8,128)(2,1)}, bf16[2,1,256,1024]{3,2,1,0:T(8,128)(2,1)}, u32[]{:S(2)}, u32[]{:S(2)}) collective-permute-start(bf16[2,1,256,1024]{3,2,1,0:T(8,128)(2,1)} %bitcast.106), channel_id=1, source_target_pairs={{0,8},{4,20},{8,0},{12,28},{16,24},{20,4},{24,16},{28,12},{1,9},{5... | collective-permute-start | bytes 3145736 | tf_op jit(solution)/shard_map/ppermute | solution.py:730
  175.8 5.1 collective-permute-start.19
  178.9 4.6 collective-permute-start.20
  179.4 26.8 %collective-permute-start.17 = (bf16[2,2,256,1024]{3,2,1,0:T(8,128)(2,1)}, bf16[2,2,256,1024]{3,2,1,0:T(8,128)(2,1)S(1)}, u32[]{:S(2)}, u32[]{:S(2)}) collective-permute-start(bf16[2,2,256,1024]{3,2,1,0:T(8,128)(2,1)} %bitcast.114), channel_id=1, source_target_pairs={{0,16},{4,12},{8,24},{12,4},{16,0},{20,28},{24,8},{28,20},{1,17},{... | collective-permute-start | bytes 6291464 | tf_op jit(solution)/shard_map/ppermute | solution.py:730
  207.6 11.2 %collective-permute-start.21 = (bf16[2,2,256,1024]{3,2,1,0:T(8,128)(2,1)}, bf16[2,2,256,1024]{3,2,1,0:T(8,128)(2,1)}, u32[]{:S(2)}, u32[]{:S(2)}) collective-permute-start(bf16[2,2,256,1024]{3,2,1,0:T(8,128)(2,1)} %gate.32), channel_id=1, source_target_pairs={{0,4},{4,0},{8,12},{12,8},{16,20},{20,16},{24,28},{28,24},{1,5},{5... | collective-permute-start | bytes 6291464 | tf_op jit(solution)/shard_map/ppermute | solution.py:720
  210.8 3.4 collective-permute-start.22
  211.4 7.3 %collective-permute-start.23 = (bf16[1024,768]{1,0:T(8,128)(2,1)S(1)}, bf16[1024,768]{1,0:T(8,128)(2,1)S(1)}, u32[]{:S(2)}, u32[]{:S(2)}) collective-permute-start(bf16[1024,768]{1,0:T(8,128)(2,1)S(1)} %copy-done.27), channel_id=1, source_target_pairs={{0,4},{4,0},{8,12},{12,8},{16,20},{20,16},{24,28},{28,24},{1,5},{5... | collective-permute-start | bytes 4718600 | tf_op jit(solution)/shard_map/ppermute | solution.py:720
  211.8 31.9 %collective-permute-start.24 = (bf16[768,2048]{1,0:T(8,128)(2,1)}, bf16[768,2048]{1,0:T(8,128)(2,1)}, u32[]{:S(2)}, u32[]{:S(2)}) collective-permute-start(bf16[768,2048]{1,0:T(8,128)(2,1)} %get-tuple-element.124), channel_id=1, source_target_pairs={{0,4},{4,0},{8,12},{12,8},{16,20},{20,16},{24,28},{28,24},{1,5},{5... | collective-permute-start | bytes 9437192 | tf_op jit(solution)/shard_map/ppermute | solution.py:720
  242.7 13.5 %collective-permute-start.25 = (bf16[768,2048]{1,0:T(8,128)(2,1)}, bf16[768,2048]{1,0:T(8,128)(2,1)}, u32[]{:S(2)}, u32[]{:S(2)}) collective-permute-start(bf16[768,2048]{1,0:T(8,128)(2,1)} %get-tuple-element.126), channel_id=1, source_target_pairs={{0,4},{4,0},{8,12},{12,8},{16,20},{20,16},{24,28},{28,24},{1,5},{5... | collective-permute-start | bytes 9437192 | tf_op jit(solution)/shard_map/ppermute | solution.py:720
  255.2 26.9 %collective-permute-start.28 = (bf16[1,2,256,2048]{3,2,1,0:T(8,128)(2,1)}, bf16[1,2,256,2048]{3,2,1,0:T(8,128)(2,1)S(1)}, u32[]{:S(2)}, u32[]{:S(2)}) collective-permute-start(bf16[1,2,256,2048]{3,2,1,0:T(8,128)(2,1)} %get-tuple-element.125.refs_9_), channel_id=1, source_target_pairs={{0,8},{4,20},{8,0},{12,28},{16,24},{20,4},{24,16},{28,12},{1,9},{5... | collective-permute-start | bytes 6291464 | tf_op jit(solution)/shard_map/ppermute | solution.py:730
  269.3 6.3 %collective-permute-start.26 = (bf16[768,512]{1,0:T(8,128)(2,1)}, bf16[768,512]{1,0:T(8,128)(2,1)S(1)}, u32[]{:S(2)}, u32[]{:S(2)}) collective-permute-start(bf16[768,512]{1,0:T(8,128)(2,1)} %get-tuple-element.132), channel_id=1, source_target_pairs={{0,4},{4,0},{8,12},{12,8},{16,20},{20,16},{24,28},{28,24},{1,5},{5... | collective-permute-start | bytes 2359304 | tf_op jit(solution)/shard_map/ppermute | solution.py:720
  270.9 2.6 collective-permute-start.27
  287.5 17.9 %collective-permute-start.29 = (bf16[1,1,256,2048]{3,2,1,0:T(8,128)(2,1)}, bf16[1,1,256,2048]{3,2,1,0:T(8,128)(2,1)S(1)}, u32[]{:S(2)}, u32[]{:S(2)}) collective-permute-start(bf16[1,1,256,2048]{3,2,1,0:T(8,128)(2,1)} %get-tuple-element.137.refs_5_), channel_id=1, source_target_pairs={{0,16},{4,12},{8,24},{12,4},{16,0},{20,28},{24,8},{28,20},{1,17},{... | collective-permute-start | bytes 3145736 | tf_op jit(solution)/shard_map/ppermute | solution.py:730
  300.0 40.4 %collective-permute-start.31 = (bf16[1,2,256,2048]{3,2,1,0:T(8,128)(2,1)}, bf16[1,2,256,2048]{3,2,1,0:T(8,128)(2,1)S(1)}, u32[]{:S(2)}, u32[]{:S(2)}) collective-permute-start(bf16[1,2,256,2048]{3,2,1,0:T(8,128)(2,1)} %get-tuple-element.138.refs_6_), channel_id=1, source_target_pairs={{0,8},{4,20},{8,0},{12,28},{16,24},{20,4},{24,16},{28,12},{1,9},{5... | collective-permute-start | bytes 6291464 | tf_op jit(solution)/shard_map/ppermute | solution.py:730
  303.4 29.9 %collective-permute-start.30 = (bf16[2,8,80,128]{3,2,1,0:T(8,128)(2,1)}, bf16[2,8,80,128]{3,2,1,0:T(8,128)(2,1)S(1)}, u32[]{:S(2)}, u32[]{:S(2)}) collective-permute-start(bf16[2,8,80,128]{3,2,1,0:T(8,128)(2,1)} %get-tuple-element.219), channel_id=1, source_target_pairs={{0,8},{4,12},{8,0},{12,4},{16,24},{20,28},{24,16},{28,20},{1,9},{5... | collective-permute-start | bytes 983048 | tf_op jit(solution)/shard_map/ppermute | solution.py:720
  303.9 35.5 %collective-permute-start.32 = (bf16[1,2,256,512]{3,2,1,0:T(8,128)(2,1)}, bf16[1,2,256,512]{3,2,1,0:T(8,128)(2,1)S(1)}, u32[]{:S(2)}, u32[]{:S(2)}) collective-permute-start(bf16[1,2,256,512]{3,2,1,0:T(8,128)(2,1)} %get-tuple-element.134.refs_4_), channel_id=1, source_target_pairs={{0,8},{4,20},{8,0},{12,28},{16,24},{20,4},{24,16},{28,12},{1,9},{5... | collective-permute-start | bytes 1572872 | tf_op jit(solution)/shard_map/ppermute | solution.py:730
  309.4 51.3 %collective-permute-start.36 = (bf16[2,32,2048]{2,1,0:T(8,128)(2,1)}, bf16[2,32,2048]{2,1,0:T(8,128)(2,1)S(1)}, u32[]{:S(2)}, u32[]{:S(2)}) collective-permute-start(bf16[2,32,2048]{2,1,0:T(8,128)(2,1)} %get-tuple-element.141.refs_7_), channel_id=1, source_target_pairs={{0,1},{1,0},{2,3},{3,2},{4,5},{5,4},{6,7},{7,6},{8,9},{9,8},{10,11... | collective-permute-start | bytes 786440 | tf_op jit(solution)/shard_map/ppermute | solution.py:720
  310.8 49.9 %collective-permute-start.37 = (bf16[2,32,2048]{2,1,0:T(8,128)(2,1)}, bf16[2,32,2048]{2,1,0:T(8,128)(2,1)S(1)}, u32[]{:S(2)}, u32[]{:S(2)}) collective-permute-start(bf16[2,32,2048]{2,1,0:T(8,128)(2,1)} %get-tuple-element.142.refs_8_), channel_id=1, source_target_pairs={{0,2},{1,3},{2,0},{3,1},{4,6},{5,7},{6,4},{7,5},{8,10},{9,11},{10,... | collective-permute-start | bytes 786440 | tf_op jit(solution)/shard_map/ppermute | solution.py:720
  333.3 27.5 %collective-permute-start.38 = (bf16[2,32,2048]{2,1,0:T(8,128)(2,1)S(1)}, bf16[2,32,2048]{2,1,0:T(8,128)(2,1)S(1)}, u32[]{:S(2)}, u32[]{:S(2)}) collective-permute-start(bf16[2,32,2048]{2,1,0:T(8,128)(2,1)S(1)} %copy-done.70), channel_id=1, source_target_pairs={{0,3},{1,2},{2,1},{3,0},{4,7},{5,6},{6,5},{7,4},{8,11},{9,10},{10,... | collective-permute-start | bytes 786440 | tf_op jit(solution)/shard_map/ppermute | solution.py:720
  339.5 20.3 %collective-permute-start.33 = (bf16[2,8,80,128]{3,2,1,0:T(8,128)(2,1)S(1)}, bf16[2,8,80,128]{3,2,1,0:T(8,128)(2,1)S(1)}, u32[]{:S(2)}, u32[]{:S(2)}) collective-permute-start(bf16[2,8,80,128]{3,2,1,0:T(8,128)(2,1)S(1)} %get-tuple-element.213), channel_id=1, source_target_pairs={{0,16},{4,20},{8,24},{12,28},{16,0},{20,4},{24,8},{28,12},{1,17},{... | collective-permute-start | bytes 983048 | tf_op jit(solution)/shard_map/ppermute | solution.py:720
  346.5 19.7 %collective-permute-start.34 = (bf16[1,1,256,2048]{3,2,1,0:T(8,128)(2,1)}, bf16[1,1,256,2048]{3,2,1,0:T(8,128)(2,1)S(1)}, u32[]{:S(2)}, u32[]{:S(2)}) collective-permute-start(bf16[1,1,256,2048]{3,2,1,0:T(8,128)(2,1)} %get-tuple-element.147.refs_7_), channel_id=1, source_target_pairs={{0,16},{4,12},{8,24},{12,4},{16,0},{20,28},{24,8},{28,20},{1,17},{... | collective-permute-start | bytes 3145736 | tf_op jit(solution)/shard_map/ppermute | solution.py:730
  359.7 6.4 %collective-permute-start.35 = (bf16[1,1,256,512]{3,2,1,0:T(8,128)(2,1)S(1)}, bf16[1,1,256,512]{3,2,1,0:T(8,128)(2,1)S(1)}, u32[]{:S(2)}, u32[]{:S(2)}) collective-permute-start(bf16[1,1,256,512]{3,2,1,0:T(8,128)(2,1)S(1)} %copy-done.71), channel_id=1, source_target_pairs={{0,16},{4,12},{8,24},{12,4},{16,0},{20,28},{24,8},{28,20},{1,17},{... | collective-permute-start | bytes 786440 | tf_op jit(solution)/shard_map/ppermute | solution.py:730
  375.2 23.9 %collective-permute-start.39 = (bf16[3,768,512]{2,1,0:T(8,128)(2,1)}, bf16[3,768,512]{2,1,0:T(8,128)(2,1)S(1)}, u32[]{:S(2)}, u32[]{:S(2)}) collective-permute-start(bf16[3,768,512]{2,1,0:T(8,128)(2,1)} %get-tuple-element.156.refs_1_), channel_id=1, source_target_pairs={{0,4},{4,0},{8,12},{12,8},{16,20},{20,16},{24,28},{28,24},{1,5},{5... | collective-permute-start | bytes 7077896 | tf_op jit(solution)/shard_map/ppermute | solution.py:720
  378.8 17.1 %collective-permute-start.40 = (bf16[2,32,2560]{2,1,0:T(8,128)(2,1)}, bf16[2,32,2560]{2,1,0:T(8,128)(2,1)S(1)}, u32[]{:S(2)}, u32[]{:S(2)}) collective-permute-start(bf16[2,32,2560]{2,1,0:T(8,128)(2,1)} %get-tuple-element.163.refs_8_), channel_id=1, source_target_pairs={{0,1},{1,0},{2,3},{3,2},{4,5},{5,4},{6,7},{7,6},{8,9},{9,8},{10,11... | collective-permute-start | bytes 983048 | tf_op jit(solution)/shard_map/ppermute | solution.py:720
  379.6 18.7 %collective-permute-start.41 = (bf16[2,32,2560]{2,1,0:T(8,128)(2,1)}, bf16[2,32,2560]{2,1,0:T(8,128)(2,1)S(1)}, u32[]{:S(2)}, u32[]{:S(2)}) collective-permute-start(bf16[2,32,2560]{2,1,0:T(8,128)(2,1)} %get-tuple-element.164.refs_9_), channel_id=1, source_target_pairs={{0,2},{1,3},{2,0},{3,1},{4,6},{5,7},{6,4},{7,5},{8,10},{9,11},{10,... | collective-permute-start | bytes 983048 | tf_op jit(solution)/shard_map/ppermute | solution.py:720
  409.9 21.6 %collective-permute-start.45 = (bf16[3,2,256,512]{3,2,1,0:T(8,128)(2,1)}, bf16[3,2,256,512]{3,2,1,0:T(8,128)(2,1)S(1)}, u32[]{:S(2)}, u32[]{:S(2)}) collective-permute-start(bf16[3,2,256,512]{3,2,1,0:T(8,128)(2,1)} %get-tuple-element.171.refs_8_), channel_id=1, source_target_pairs={{0,8},{4,20},{8,0},{12,28},{16,24},{20,4},{24,16},{28,12},{1,9},{5... | collective-permute-start | bytes 4718600 | tf_op jit(solution)/shard_map/ppermute | solution.py:730
  412.2 12.3 %collective-permute-start.42 = (bf16[2,32,2560]{2,1,0:T(8,128)(2,1)S(1)}, bf16[2,32,2560]{2,1,0:T(8,128)(2,1)S(1)}, u32[]{:S(2)}, u32[]{:S(2)}) collective-permute-start(bf16[2,32,2560]{2,1,0:T(8,128)(2,1)S(1)} %copy-done.58), channel_id=1, source_target_pairs={{0,3},{1,2},{2,1},{3,0},{4,7},{5,6},{6,5},{7,4},{8,11},{9,10},{10,... | collective-permute-start | bytes 983048 | tf_op jit(solution)/shard_map/ppermute | solution.py:720
  424.5 1.5 collective-permute-start.43
  426.7 4.2 collective-permute-start.44
  436.8 19.6 %collective-permute-start.49 = (bf16[3,1,256,512]{3,2,1,0:T(8,128)(2,1)}, bf16[3,1,256,512]{3,2,1,0:T(8,128)(2,1)S(1)}, u32[]{:S(2)}, u32[]{:S(2)}) collective-permute-start(bf16[3,1,256,512]{3,2,1,0:T(8,128)(2,1)} %get-tuple-element.177.refs_1_), channel_id=1, source_target_pairs={{0,16},{4,12},{8,24},{12,4},{16,0},{20,28},{24,8},{28,20},{1,17},{... | collective-permute-start | bytes 2359304 | tf_op jit(solution)/shard_map/ppermute | solution.py:730
  437.8 14.9 %collective-permute-start.62 = (f32[1,32,2048]{2,1,0:T(8,128)S(1)}, f32[1,32,2048]{2,1,0:T(8,128)S(1)}, u32[]{:S(2)}, u32[]{:S(2)}) collective-permute-start(f32[1,32,2048]{2,1,0:T(8,128)S(1)} %constant_dynamic-slice_fusion.5), channel_id=1, source_target_pairs={{0,4},{4,0},{8,12},{12,8},{16,20},{20,16},{24,28},{28,24},{1,5},{5... | collective-permute-start | bytes 786440 | tf_op jit(solution)/shard_map/ppermute | solution.py:720
  437.9 11.5 %collective-permute-start.46 = (f32[4,1024]{1,0:T(4,128)}, f32[4,1024]{1,0:T(4,128)S(1)}, u32[]{:S(2)}, u32[]{:S(2)}) collective-permute-start(f32[4,1024]{1,0:T(4,128)} %gate.39), channel_id=1, source_target_pairs={{0,16},{4,20},{8,24},{12,28},{16,0},{20,4},{24,8},{28,12},{1,17},{... | collective-permute-start | bytes 49160 | tf_op jit(solution)/shard_map/ppermute | solution.py:720
  450.1 4.3 collective-permute-start.47
  454.5 12.0 %collective-permute-start.48 = (f32[4,1024]{1,0:T(4,128)S(1)}, f32[4,1024]{1,0:T(4,128)S(1)}, u32[]{:S(2)}, u32[]{:S(2)}) collective-permute-start(f32[4,1024]{1,0:T(4,128)S(1)} %add.279), channel_id=1, source_target_pairs={{0,2},{1,3},{2,0},{3,1},{4,6},{5,7},{6,4},{7,5},{8,10},{9,11},{10,... | collective-permute-start | bytes 49160 | tf_op jit(solution)/shard_map/ppermute | solution.py:720
  460.1 7.8 %collective-permute-start.50 = (bf16[6,32,512]{2,1,0:T(8,128)(2,1)}, bf16[6,32,512]{2,1,0:T(8,128)(2,1)S(1)}, u32[]{:S(2)}, u32[]{:S(2)}) collective-permute-start(bf16[6,32,512]{2,1,0:T(8,128)(2,1)} %get-tuple-element.180), channel_id=1, source_target_pairs={{0,1},{1,0},{2,3},{3,2},{4,5},{5,4},{6,7},{7,6},{8,9},{9,8},{10,11... | collective-permute-start | bytes 589832 | tf_op jit(solution)/shard_map/ppermute | solution.py:720
  460.5 11.6 %collective-permute-start.51 = (bf16[6,32,512]{2,1,0:T(8,128)(2,1)}, bf16[6,32,512]{2,1,0:T(8,128)(2,1)S(1)}, u32[]{:S(2)}, u32[]{:S(2)}) collective-permute-start(bf16[6,32,512]{2,1,0:T(8,128)(2,1)} %get-tuple-element.181), channel_id=1, source_target_pairs={{0,2},{1,3},{2,0},{3,1},{4,6},{5,7},{6,4},{7,5},{8,10},{9,11},{10,... | collective-permute-start | bytes 589832 | tf_op jit(solution)/shard_map/ppermute | solution.py:720
  463.2 8.9 %collective-permute-start.52 = (bf16[6,32,512]{2,1,0:T(8,128)(2,1)}, bf16[6,32,512]{2,1,0:T(8,128)(2,1)S(1)}, u32[]{:S(2)}, u32[]{:S(2)}) collective-permute-start(bf16[6,32,512]{2,1,0:T(8,128)(2,1)} %get-tuple-element.182), channel_id=1, source_target_pairs={{0,3},{1,2},{2,1},{3,0},{4,7},{5,6},{6,5},{7,4},{8,11},{9,10},{10,... | collective-permute-start | bytes 589832 | tf_op jit(solution)/shard_map/ppermute | solution.py:720
  465.2 21.9 %collective-permute-start.61 = (f32[1,32,2560]{2,1,0:T(8,128)}, f32[1,32,2560]{2,1,0:T(8,128)}, u32[]{:S(2)}, u32[]{:S(2)}) collective-permute-start(f32[1,32,2560]{2,1,0:T(8,128)} %constant_dynamic-slice_fusion.4), channel_id=1, source_target_pairs={{0,4},{4,0},{8,12},{12,8},{16,20},{20,16},{24,28},{28,24},{1,5},{5... | collective-permute-start | bytes 983048 | tf_op jit(solution)/shard_map/ppermute | solution.py:720
  475.3 6.5 %collective-permute-start.53 = (f32[8,128]{1,0:T(8,128)S(1)}, f32[8,128]{1,0:T(8,128)S(1)}, u32[]{:S(2)}, u32[]{:S(2)}) collective-permute-start(f32[8,128]{1,0:T(8,128)S(1)} %broadcast_in_dim.37), channel_id=1, source_target_pairs={{0,1},{1,0},{2,3},{3,2},{4,5},{5,4},{6,7},{7,6},{8,9},{9,8},{10,11... | collective-permute-start | bytes 12296 | tf_op jit(solution)/shard_map/ppermute | solution.py:720
  478.0 4.5 collective-permute-start.54
  478.2 5.4 %collective-permute-start.55 = (f32[8,128]{1,0:T(8,128)S(1)}, f32[8,128]{1,0:T(8,128)S(1)}, u32[]{:S(2)}, u32[]{:S(2)}) collective-permute-start(f32[8,128]{1,0:T(8,128)S(1)} %broadcast_in_dim.37), channel_id=1, source_target_pairs={{0,3},{1,2},{2,1},{3,0},{4,7},{5,6},{6,5},{7,4},{8,11},{9,10},{10,... | collective-permute-start | bytes 12296 | tf_op jit(solution)/shard_map/ppermute | solution.py:720
  483.6 4.6 collective-permute-start.56
  484.8 3.6 collective-permute-start.57
  486.1 4.5 collective-permute-start.58
  491.3 6.9 %collective-permute-start.60 = (f32[3,32,512]{2,1,0:T(8,128)}, f32[3,32,512]{2,1,0:T(8,128)}, u32[]{:S(2)}, u32[]{:S(2)}) collective-permute-start(f32[3,32,512]{2,1,0:T(8,128)} %dynamic-slice_bitcast_fusion), channel_id=1, source_target_pairs={{0,4},{4,0},{8,12},{12,8},{16,20},{20,16},{24,28},{28,24},{1,5},{5... | collective-permute-start | bytes 589832 | tf_op jit(solution)/shard_map/ppermute | solution.py:720
  (73 other events, 458.1 us)
Sparse Core Ops, SparseCore 0:
  62.1 28.7 all-gather.2
  120.6 28.8 all-gather.4
